TPU v7x, 512 devices: a whole 4x8x8 slice. The times are simulated.
512 devices in a mesh: cluster: 128 (over z, y, core), rep: 4 (over x).
Axes of the slice: x: 4, y: 8, z: 8, core: 2. Of those that a mesh axis runs over, the one named last changes fastest.
Arguments:
- embeddings: float32 [131072, 1024], P(('cluster', 'rep'))
- cluster_sizes: int32 [128], P('cluster'), may hold values from 256 to 1024, as said below
- offsets: int32 [2, 128], P(None, 'cluster'), may hold values from 1 to 3, as said below
Outputs:
- best_rows: float32 [131072], P(('cluster', 'rep'))
Inputs may be any that keep to these rules, and one draw needn't show every extreme that they name: `cluster_sizes`: every cluster has at least 256 rows in use; some cluster is full and some has exactly 256. A cluster's offsets in the 2 rounds are distinct; some cluster has offset 3 in the first round.
All inputs are finite; a program needn't handle non-finite values.
Results may differ from a plain program's by a relative error of at most 0.0003.
Values may be sent and summed in bfloat16 or wider, within the bound.
No kernel may reach another device: no remote copies, remote signals or barrier semaphores. Data moves between devices by JAX's collectives and lax.ppermute only.
A program may use at most 64 MiB of HBM per device.

v0:
```python
import jax
import jax.numpy as jnp
from jax import lax
from jax.sharding import PartitionSpec as P

SPAN = 3


def from_behind(block, axis, distance):
    devices = range(lax.axis_size(axis))
    route = [((i - distance) % len(devices), i) for i in devices]
    return lax.ppermute(block, axis, route)


def score_tile(unit_rows, own_valid, partner_rows, partner_size):
    scores = lax.dot_general(
        unit_rows, partner_rows, (((1,), (1,)), ((), ())), preferred_element_type=jnp.float32
    )
    column_ids = jnp.arange(partner_rows.shape[0], dtype=jnp.int32)
    allowed = own_valid[:, None] & (column_ids < partner_size[0])[None, :]
    return jnp.where(allowed, scores, -4.0)


def chain_whole(payload, direction):
    found = []
    for distance in range(SPAN):
        payload = from_behind((payload[0], payload[1], payload[2]), "cluster", direction)
        found.append(payload)
    return found


def pick_partner(found, offset):
    chosen_rows, chosen_size = (found[0][0], found[0][1])
    for distance in range(1, len(found)):
        matched = offset == distance + 1
        chosen_rows = jnp.where(matched, found[distance][0], chosen_rows)
        chosen_size = jnp.where(matched, found[distance][1], chosen_size)
    return (chosen_rows, chosen_size)


def pair_scores(unit_rows, own_valid, partner_rows, partner_size):
    return score_tile(unit_rows, own_valid, partner_rows, partner_size)


def fetch_chain(cluster_sizes, offsets, own_cluster, direction):
    return chain_whole((own_cluster, cluster_sizes, offsets), direction)


def shards(embeddings, cluster_sizes, offsets):
    rows_dev = embeddings.shape[0]
    rep_index = lax.axis_index("rep")
    row_norms = jnp.sqrt(jnp.sum(embeddings * embeddings, axis=1, keepdims=True) + 1e-06)
    unit_rows = (embeddings / row_norms).astype(jnp.bfloat16)
    row_ids = rep_index * rows_dev + jnp.arange(rows_dev, dtype=jnp.int32)
    own_valid = row_ids < cluster_sizes[0]
    own_cluster = lax.all_gather(unit_rows, "rep", axis=0, tiled=True)
    forward = fetch_chain(cluster_sizes, offsets, own_cluster, -1)
    row_best = jnp.full((rows_dev,), -4.0, jnp.float32)
    column_list = []
    for round_index in range(offsets.shape[0]):
        offset = offsets[round_index, 0]
        partner_rows, partner_size = pick_partner(forward, offset)
        scores = pair_scores(unit_rows, own_valid, partner_rows, partner_size)
        row_best = jnp.maximum(row_best, jnp.max(scores, axis=1))
        column_list.append(jnp.max(scores, axis=0))
    column_best = lax.pmax(jnp.stack(column_list, axis=0), "rep")
    carried = (column_best, offsets[:, 0])
    returned = jnp.full((column_best.shape[1],), -4.0, jnp.float32)
    for distance in range(SPAN):
        carried = from_behind((carried[0], carried[1]), "cluster", 1)
        aimed = carried[1] == distance + 1
        taken = jnp.where(aimed[:, None], carried[0], -4.0)
        returned = jnp.maximum(returned, jnp.max(taken, axis=0))
    row_best = jnp.maximum(
        row_best, lax.dynamic_slice_in_dim(returned, rep_index * rows_dev, rows_dev)
    )
    return jnp.where(own_valid, row_best, 0.0)


def solution(mesh):
    return jax.shard_map(
        shards,
        mesh=mesh,
        in_specs=(P(("cluster", "rep"), None), P("cluster"), P(None, "cluster")),
        out_specs=P(("cluster", "rep")),
        check_vma=False,
    )
```

profile of v0, /device:TPU:2, one launch (start us, length us, event | category | flops | bytes accessed | tf_op | source)
XLA Modules:
  0.0 218.5 jit_solution(455397985141643677)
XLA Ops:
  7.9 2.2 divide_convert_fusion
  10.1 40.0 %all-gather.2.cloned.1.call-done = bf16[1024,1024]{1,0:T(8,128)(2,1)} async-done(((bf16[256,1024]{1,0:T(8,128)(2,1)}), bf16[1024,1024]{1,0:T(8,128)(2,1)}) %all-gather.2.cloned.1.call-update) | async-done | bytes 2097168 | tf_op jit(solution)/shard_map/all_gather | solution.py:56
  50.2 7.6 %collective-permute-start.3 = (bf16[1024,1024]{1,0:T(8,128)(2,1)}, bf16[1024,1024]{1,0:T(8,128)(2,1)S(1)}, u32[]{:S(2)}, u32[]{:S(2)}) collective-permute-start(bf16[1024,1024]{1,0:T(8,128)(2,1)} %all-gather.2.cloned.1.call-done), channel_id=1, source_target_pairs={{4,0},{8,4},{12,8},{16,12},{20,16},{24,20},{28,24},{32,28},{36,32}... | collective-permute-start | bytes 6291464 | tf_op jit(solution)/shard_map/ppermute | solution.py:12
  57.7 23.8 %collective-permute-done.3 = bf16[1024,1024]{1,0:T(8,128)(2,1)S(1)} collective-permute-done((bf16[1024,1024]{1,0:T(8,128)(2,1)}, bf16[1024,1024]{1,0:T(8,128)(2,1)S(1)}, u32[]{:S(2)}, u32[]{:S(2)}) %collective-permute-start.3) | collective-permute-done | bytes 2097184 | tf_op jit(solution)/shard_map/ppermute | solution.py:12
  81.6 7.0 %collective-permute-start.4 = (bf16[1024,1024]{1,0:T(8,128)(2,1)S(1)}, bf16[1024,1024]{1,0:T(8,128)(2,1)}, u32[]{:S(2)}, u32[]{:S(2)}) collective-permute-start(bf16[1024,1024]{1,0:T(8,128)(2,1)S(1)} %collective-permute-done.3), channel_id=1, source_target_pairs={{4,0},{8,4},{12,8},{16,12},{20,16},{24,20},{28,24},{32,28},{36,32}... | collective-permute-start | bytes 6291464 | tf_op jit(solution)/shard_map/ppermute | solution.py:12
  88.6 23.5 %collective-permute-done.4 = bf16[1024,1024]{1,0:T(8,128)(2,1)} collective-permute-done((bf16[1024,1024]{1,0:T(8,128)(2,1)S(1)}, bf16[1024,1024]{1,0:T(8,128)(2,1)}, u32[]{:S(2)}, u32[]{:S(2)}) %collective-permute-start.4) | collective-permute-done | bytes 2097184 | tf_op jit(solution)/shard_map/ppermute | solution.py:12
  112.1 7.2 %collective-permute-start.5 = (bf16[1024,1024]{1,0:T(8,128)(2,1)}, bf16[1024,1024]{1,0:T(8,128)(2,1)}, u32[]{:S(2)}, u32[]{:S(2)}) collective-permute-start(bf16[1024,1024]{1,0:T(8,128)(2,1)} %collective-permute-done.4), channel_id=1, source_target_pairs={{4,0},{8,4},{12,8},{16,12},{20,16},{24,20},{28,24},{32,28},{36,32}... | collective-permute-start | bytes 6291464 | tf_op jit(solution)/shard_map/ppermute | solution.py:12
  119.4 1.9 collective-permute-start
  121.3 2.4 %collective-permute-start.6 = (s32[2]{0:T(128)S(1)}, s32[2]{0:T(128)S(1)}, u32[]{:S(2)}, u32[]{:S(2)}) collective-permute-start(s32[2]{0:T(128)S(1)} %bitcast.20), channel_id=1, source_target_pairs={{508,0},{0,4},{4,8},{8,12},{12,16},{16,20},{20,24},{24,28},{28,32}... | collective-permute-start | bytes 32 | tf_op jit(solution)/shard_map/ppermute | solution.py:12
  127.5 15.7 %collective-permute-done = s32[1]{0:T(128)} collective-permute-done((s32[1]{0:T(128)}, s32[1]{0:T(128)}, u32[]{:S(2)}, u32[]{:S(2)}) %collective-permute-start) | collective-permute-done | bytes 36 | tf_op jit(solution)/shard_map/ppermute | solution.py:12
  143.2 7.2 %collective-permute-start.1 = (s32[1]{0:T(128)}, s32[1]{0:T(128)}, u32[]{:S(2)}, u32[]{:S(2)}) collective-permute-start(s32[1]{0:T(128)} %collective-permute-done), channel_id=1, source_target_pairs={{4,0},{8,4},{12,8},{16,12},{20,16},{24,20},{28,24},{32,28},{36,32}... | collective-permute-start | bytes 20 | tf_op jit(solution)/shard_map/ppermute | solution.py:12
  151.7 6.8 %collective-permute-start.2 = (s32[1]{0:T(128)}, s32[1]{0:T(128)}, u32[]{:S(2)}, u32[]{:S(2)}) collective-permute-start(s32[1]{0:T(128)} %collective-permute-done.1), channel_id=1, source_target_pairs={{4,0},{8,4},{12,8},{16,12},{20,16},{24,20},{28,24},{32,28},{36,32}... | collective-permute-start | bytes 20 | tf_op jit(solution)/shard_map/ppermute | solution.py:12
  161.1 1.9 collective-permute-start.8
  164.4 5.0 %collective-permute-done.8 = s32[2]{0:T(128)S(1)} collective-permute-done((s32[2]{0:T(128)S(1)}, s32[2]{0:T(128)S(1)}, u32[]{:S(2)}, u32[]{:S(2)}) %collective-permute-start.8) | collective-permute-done | bytes 40 | tf_op jit(solution)/shard_map/ppermute | solution.py:12
  169.3 1.9 collective-permute-start.10
  171.3 2.8 %fusion.16 = (f32[256]{0:T(256)S(1)}, f32[1024]{0:T(1024)S(1)}) fusion(bf16[256,1024]{1,0:T(8,128)(2,1)} %divide_convert_fusion, bf16[1024,1024]{1,0:T(8,128)(2,1)} %collective-permute-done.5, bf16[1024,1024]{1,0:T(8,128)(2,1)} %collective-permute-done.4, bf16[1024,1024]{1,0:T(8,128)(2,1)S(1)} %collective-permute-done.3, pred[]{:T(512)} %bitcast.5, ...), kind=kOutput, calls=%fused_computation.27 | convolution fusion | flops 540015360 | bytes 6822146 | tf_op jit(solution)/shard_map/dot_general | solution.py:16
  174.1 2.6 %fusion.17 = (f32[256]{0:T(256)S(1)}, f32[1024]{0:T(1024)S(1)}) fusion(bf16[256,1024]{1,0:T(8,128)(2,1)S(1)} %copy-done, bf16[1024,1024]{1,0:T(8,128)(2,1)} %collective-permute-done.5, bf16[1024,1024]{1,0:T(8,128)(2,1)} %collective-permute-done.4, bf16[1024,1024]{1,0:T(8,128)(2,1)S(1)} %collective-permute-done.3, pred[]{:T(512)} %bitcast.10, pred[]{:T(512)} %bitcast.9, ...), kind=kOutput, calls=%fused_computation.28 | convolution fusion | flops 540015360 | bytes 6822146 | tf_op jit(solution)/shard_map/dot_general | solution.py:16
  176.8 9.3 %pmax.7 = f32[2,1024]{1,0:T(2,128)S(1)} all-reduce(f32[2,1024]{1,0:T(2,128)S(1)} %pad_maximum_fusion), channel_id=1, replica_groups=mesh['cluster'=128,'rep'=4] {'rep'}, use_global_device_ids=true, to_apply=%region_5.6 | all-reduce | flops 2048 | bytes 16384 | tf_op jit(solution)/shard_map/pmax | solution.py:66
  186.1 1.9 collective-permute-start.7
  188.0 6.3 %collective-permute-done.7 = f32[2,1024]{1,0:T(2,128)S(1)} collective-permute-done((f32[2,1024]{1,0:T(2,128)S(1)}, f32[2,1024]{1,0:T(2,128)S(1)}, u32[]{:S(2)}, u32[]{:S(2)}) %collective-permute-start.7) | collective-permute-done | bytes 8224 | tf_op jit(solution)/shard_map/ppermute | solution.py:12
  194.4 1.9 collective-permute-start.9
  196.4 6.3 %collective-permute-done.9 = f32[2,1024]{1,0:T(2,128)S(1)} collective-permute-done((f32[2,1024]{1,0:T(2,128)S(1)}, f32[2,1024]{1,0:T(2,128)S(1)}, u32[]{:S(2)}, u32[]{:S(2)}) %collective-permute-start.9) | collective-permute-done | bytes 8224 | tf_op jit(solution)/shard_map/ppermute | solution.py:12
  202.7 1.9 collective-permute-start.11
  204.7 6.3 %collective-permute-done.11 = f32[2,1024]{1,0:T(2,128)S(1)} collective-permute-done((f32[2,1024]{1,0:T(2,128)S(1)}, f32[2,1024]{1,0:T(2,128)S(1)}, u32[]{:S(2)}, u32[]{:S(2)}) %collective-permute-start.11) | collective-permute-done | bytes 8224 | tf_op jit(solution)/shard_map/ppermute | solution.py:12
  (26 shorter events, 4.3 us)
Async XLA Ops:
  6.5 114.8 %copy-start.1 = (s32[2,1]{0,1:T(1,128)S(1)}, s32[2,1]{0,1:T(1,128)}, u32[]{:S(2)}) copy-start(s32[2,1]{0,1:T(1,128)} %param.5) | copy-start | bytes 28
  6.5 43.6 %all-gather.2.cloned.1.call-start = ((), (), s32[]{:S(2)}) async-start(), calls=%async_computation | async-start | bytes 2621440 | tf_op jit(solution)/shard_map/all_gather | solution.py:56
  50.2 31.4 %collective-permute-start.3 = (bf16[1024,1024]{1,0:T(8,128)(2,1)}, bf16[1024,1024]{1,0:T(8,128)(2,1)S(1)}, u32[]{:S(2)}, u32[]{:S(2)}) collective-permute-start(bf16[1024,1024]{1,0:T(8,128)(2,1)} %all-gather.2.cloned.1.call-done), channel_id=1, source_target_pairs={{4,0},{8,4},{12,8},{16,12},{20,16},{24,20},{28,24},{32,28},{36,32}... | collective-permute-start | bytes 6291464 | tf_op jit(solution)/shard_map/ppermute | solution.py:12
  81.6 30.6 %collective-permute-start.4 = (bf16[1024,1024]{1,0:T(8,128)(2,1)S(1)}, bf16[1024,1024]{1,0:T(8,128)(2,1)}, u32[]{:S(2)}, u32[]{:S(2)}) collective-permute-start(bf16[1024,1024]{1,0:T(8,128)(2,1)S(1)} %collective-permute-done.3), channel_id=1, source_target_pairs={{4,0},{8,4},{12,8},{16,12},{20,16},{24,20},{28,24},{32,28},{36,32}... | collective-permute-start | bytes 6291464 | tf_op jit(solution)/shard_map/ppermute | solution.py:12
  112.1 59.1 %collective-permute-start.5 = (bf16[1024,1024]{1,0:T(8,128)(2,1)}, bf16[1024,1024]{1,0:T(8,128)(2,1)}, u32[]{:S(2)}, u32[]{:S(2)}) collective-permute-start(bf16[1024,1024]{1,0:T(8,128)(2,1)} %collective-permute-done.4), channel_id=1, source_target_pairs={{4,0},{8,4},{12,8},{16,12},{20,16},{24,20},{28,24},{32,28},{36,32}... | collective-permute-start | bytes 6291464 | tf_op jit(solution)/shard_map/ppermute | solution.py:12
  119.4 23.8 %collective-permute-start = (s32[1]{0:T(128)}, s32[1]{0:T(128)}, u32[]{:S(2)}, u32[]{:S(2)}) collective-permute-start(s32[1]{0:T(128)} %param.4), channel_id=1, source_target_pairs={{4,0},{8,4},{12,8},{16,12},{20,16},{24,20},{28,24},{32,28},{36,32}... | collective-permute-start | bytes 20 | tf_op jit(solution)/shard_map/ppermute | solution.py:12
  121.3 39.8 %collective-permute-start.6 = (s32[2]{0:T(128)S(1)}, s32[2]{0:T(128)S(1)}, u32[]{:S(2)}, u32[]{:S(2)}) collective-permute-start(s32[2]{0:T(128)S(1)} %bitcast.20), channel_id=1, source_target_pairs={{508,0},{0,4},{4,8},{8,12},{12,16},{16,20},{20,24},{24,28},{28,32}... | collective-permute-start | bytes 32 | tf_op jit(solution)/shard_map/ppermute | solution.py:12
  143.2 8.5 %collective-permute-start.1 = (s32[1]{0:T(128)}, s32[1]{0:T(128)}, u32[]{:S(2)}, u32[]{:S(2)}) collective-permute-start(s32[1]{0:T(128)} %collective-permute-done), channel_id=1, source_target_pairs={{4,0},{8,4},{12,8},{16,12},{20,16},{24,20},{28,24},{32,28},{36,32}... | collective-permute-start | bytes 20 | tf_op jit(solution)/shard_map/ppermute | solution.py:12
  151.7 11.3 %collective-permute-start.2 = (s32[1]{0:T(128)}, s32[1]{0:T(128)}, u32[]{:S(2)}, u32[]{:S(2)}) collective-permute-start(s32[1]{0:T(128)} %collective-permute-done.1), channel_id=1, source_target_pairs={{4,0},{8,4},{12,8},{16,12},{20,16},{24,20},{28,24},{32,28},{36,32}... | collective-permute-start | bytes 20 | tf_op jit(solution)/shard_map/ppermute | solution.py:12
  161.1 8.2 %collective-permute-start.8 = (s32[2]{0:T(128)S(1)}, s32[2]{0:T(128)S(1)}, u32[]{:S(2)}, u32[]{:S(2)}) collective-permute-start(s32[2]{0:T(128)S(1)} %collective-permute-done.6), channel_id=1, source_target_pairs={{508,0},{0,4},{4,8},{8,12},{12,16},{16,20},{20,24},{24,28},{28,32}... | collective-permute-start | bytes 32 | tf_op jit(solution)/shard_map/ppermute | solution.py:12
  169.3 18.7 %collective-permute-start.10 = (s32[2]{0:T(128)S(1)}, s32[2]{0:T(128)S(1)}, u32[]{:S(2)}, u32[]{:S(2)}) collective-permute-start(s32[2]{0:T(128)S(1)} %collective-permute-done.8), channel_id=1, source_target_pairs={{508,0},{0,4},{4,8},{8,12},{12,16},{16,20},{20,24},{24,28},{28,32}... | collective-permute-start | bytes 32 | tf_op jit(solution)/shard_map/ppermute | solution.py:12
  171.3 2.8 %copy-start = (bf16[256,1024]{1,0:T(8,128)(2,1)S(1)}, bf16[256,1024]{1,0:T(8,128)(2,1)}, u32[]{:S(2)}) copy-start(bf16[256,1024]{1,0:T(8,128)(2,1)} %divide_convert_fusion) | copy-start | bytes 1572868
  186.1 8.3 %collective-permute-start.7 = (f32[2,1024]{1,0:T(2,128)S(1)}, f32[2,1024]{1,0:T(2,128)S(1)}, u32[]{:S(2)}, u32[]{:S(2)}) collective-permute-start(f32[2,1024]{1,0:T(2,128)S(1)} %pmax.7), channel_id=1, source_target_pairs={{508,0},{0,4},{4,8},{8,12},{12,16},{16,20},{20,24},{24,28},{28,32}... | collective-permute-start | bytes 24584 | tf_op jit(solution)/shard_map/ppermute | solution.py:12
  194.4 8.3 %collective-permute-start.9 = (f32[2,1024]{1,0:T(2,128)S(1)}, f32[2,1024]{1,0:T(2,128)S(1)}, u32[]{:S(2)}, u32[]{:S(2)}) collective-permute-start(f32[2,1024]{1,0:T(2,128)S(1)} %collective-permute-done.7), channel_id=1, source_target_pairs={{508,0},{0,4},{4,8},{8,12},{12,16},{16,20},{20,24},{24,28},{28,32}... | collective-permute-start | bytes 24584 | tf_op jit(solution)/shard_map/ppermute | solution.py:12
  202.7 8.3 %collective-permute-start.11 = (f32[2,1024]{1,0:T(2,128)S(1)}, f32[2,1024]{1,0:T(2,128)S(1)}, u32[]{:S(2)}, u32[]{:S(2)}) collective-permute-start(f32[2,1024]{1,0:T(2,128)S(1)} %collective-permute-done.9), channel_id=1, source_target_pairs={{508,0},{0,4},{4,8},{8,12},{12,16},{16,20},{20,24},{24,28},{28,32}... | collective-permute-start | bytes 24584 | tf_op jit(solution)/shard_map/ppermute | solution.py:12
Sparse Core Ops, SparseCore 0:
  10.3 39.8 all-gather.1
where the time goes:
time: 219 us
  waiting for transfers between devices  128 us (58%)
  starting transfers between devices  49.7 us (23%)
  between operations  20.6 us (9%)
  blocking collectives  9.32 us (4%)
  matrix products  5.46 us (2%)
  other arithmetic  4.52 us (2%)
    ppermute x12, waiting for transfers between devices, from_behind(): return lax.ppermute(block, axis, route)  88.2 us
    ppermute x12, starting transfers between devices, from_behind(): return lax.ppermute(block, axis, route)  49.7 us
    all_gather x1, waiting for transfers between devices, shards(): own_cluster = lax.all_gather(unit_rows, 'rep', axis=0, tiled=True)  40 us
    pmax x1, blocking collectives, shards(): column_best = lax.pmax(jnp.stack(column_list, axis=0), 'rep')  9.32 us
    dot_general x2, matrix products, score_tile(): lax.dot_general(unit_rows, partner_rows, (((1,), (1,)), ((), ())), prefer...  5.46 us
  transfers between devices with their start and end apart: 13, of which 9 were waited for; matrix products, arithmetic and copies ran while one was open for 3% of the time, Pallas kernels for 0%

commit v1 on v0

v1 whole, which is shorter than its diff:
```python
import jax
import jax.numpy as jnp
from jax import lax
from jax.experimental import pallas as pl
from jax.experimental.pallas import tpu as pltpu
from jax.sharding import PartitionSpec as P

SPAN = 3
META = 16
VMEM = pl.BlockSpec(memory_space=pltpu.VMEM)
SMEM = pl.BlockSpec(memory_space=pltpu.SMEM)


def norm_kernel(size_ref, offset_ref, rows_ref, unit_ref, payload_ref):
    rows, width = rows_ref.shape
    values = rows_ref[...]
    norms = jnp.sqrt(jnp.sum(values * values, axis=1, keepdims=True) + 1e-06)
    unit = (values / norms).astype(jnp.bfloat16)
    unit_ref[...] = unit
    payload_ref[0:rows, :] = unit
    used = jnp.clip(size_ref[0] - lax.axis_index("rep") * rows, 0, rows)
    line = lax.broadcasted_iota(jnp.int32, (META, width), 0)
    meta = jnp.where(line == 0, used, 0)
    for k in range(offset_ref.shape[0]):
        meta = jnp.where(line == k + 1, offset_ref[k, 0], meta)
    payload_ref[rows:, :] = meta.astype(jnp.float32).astype(jnp.bfloat16)


def neighbour_bias(offset_ref, payload_ref, delta, rows):
    meta = payload_ref[rows:, 0:128].astype(jnp.float32)
    own = jnp.bool_(False)
    theirs = jnp.zeros((1, 128), jnp.bool_)
    for k in range(offset_ref.shape[0]):
        own = own | (offset_ref[k, 0] == delta)
        theirs = theirs | (meta[k + 1 : k + 2, :] == (-delta).astype(jnp.float32))
    own_flag = jnp.where(own, 1.0, 0.0)
    flag = jnp.where(delta > 0, own_flag, jnp.where(theirs, 1.0, 0.0))
    used = meta[0:1, :] * flag
    line = lax.broadcasted_iota(jnp.int32, (rows, 128), 0).astype(jnp.float32)
    return jnp.where(line < used, 0.0, -8.0)


def maxima_kernel(offset_ref, *refs):
    pieces, payloads, best_ref = refs[:4], refs[4:-1], refs[-1]
    rows = pieces[0].shape[0]
    odd = lax.rem(lax.axis_index("cluster"), 2)
    rep = lax.axis_index("rep")
    deltas = (1 - 2 * odd, jnp.int32(2), jnp.int32(-2), 3 - 2 * odd, -1 - 2 * odd, 6 * odd - 3)
    biases = [neighbour_bias(offset_ref, p, d, rows) for p, d in zip(payloads, deltas)]
    for away, piece in enumerate(pieces):
        best = jnp.full((1, rows), -4.0, jnp.float32)
        for payload, bias in zip(payloads, biases):
            scores = lax.dot_general(
                payload[0:rows, :], piece[...], (((1,), (1,)), ((), ())), preferred_element_type=jnp.float32
            )
            wide = jnp.concatenate([bias] * (rows // 128), axis=1)
            best = jnp.maximum(best, jnp.max(scores + wide, axis=0, keepdims=True))
        best_ref[pl.ds(lax.rem(rep + away, 4), 1), :] = best


def over_cluster(block, source):
    n = lax.axis_size("cluster")
    return lax.ppermute(block, "cluster", [(source(i) % n, i) for i in range(n)])


def over_rep(block, away):
    n = lax.axis_size("rep")
    return lax.ppermute(block, "rep", [((i + away) % n, i) for i in range(n)])


def shards(embeddings, cluster_sizes, offsets):
    rows, width = embeddings.shape
    unit, payload = pl.pallas_call(
        norm_kernel,
        out_shape=(
            jax.ShapeDtypeStruct((rows, width), jnp.bfloat16),
            jax.ShapeDtypeStruct((rows + META, width), jnp.bfloat16),
        ),
        in_specs=[SMEM, SMEM, VMEM],
        out_specs=(VMEM, VMEM),
        name="unit_rows",
    )(cluster_sizes, offsets, embeddings)
    pieces = [unit] + [over_rep(unit, away) for away in (1, 2, 3)]
    ahead = over_cluster(payload, lambda i: i + 2)
    behind = over_cluster(payload, lambda i: i - 2)
    far = over_cluster(payload, lambda i: i + 3 if i % 2 else i - 3)
    mate = over_cluster(payload, lambda i: i ^ 1)
    ahead_mate = over_cluster(ahead, lambda i: i ^ 1)
    behind_mate = over_cluster(behind, lambda i: i ^ 1)
    best = pl.pallas_call(
        maxima_kernel,
        out_shape=jax.ShapeDtypeStruct((4, rows), jnp.float32),
        in_specs=[SMEM] + [VMEM] * 10,
        out_specs=VMEM,
        name="maxima",
        compiler_params=pltpu.CompilerParams(vmem_limit_bytes=32 * 1024 * 1024),
    )(offsets, *pieces, mate, ahead, behind, ahead_mate, behind_mate, far)
    row_best = jnp.max(lax.all_to_all(best, "rep", 0, 0), axis=0)
    row_ids = lax.axis_index("rep") * rows + jnp.arange(rows, dtype=jnp.int32)
    return jnp.where(row_ids < cluster_sizes[0], row_best, 0.0)


def solution(mesh):
    return jax.shard_map(
        shards,
        mesh=mesh,
        in_specs=(P(("cluster", "rep"), None), P("cluster"), P(None, "cluster")),
        out_specs=P(("cluster", "rep")),
        check_vma=False,
    )
```

time: 219 us -> 86.2 us (0.39)
  waiting for transfers between devices: 128 us -> 35.1 us
  between operations: 20.6 us -> 0.78 us
  starting transfers between devices: 49.7 us -> 39.5 us
  blocking collectives: 9.32 us -> 0 us
  Pallas kernels: 0 us -> 6.55 us
  matrix products: 5.46 us -> 0 us
  other arithmetic: 4.52 us -> 0.59 us
  local copies, waits for them, and re-layouts: 0.6 us -> 2.92 us
    ppermute x12 -> x9, waiting for transfers between devices: 88.2 us -> 31.3 us  [the longest x3 31.3 us: over_rep(): return lax.ppermute(block, 'rep', [((i + away) % n, i) for i in range(n)])]
    all_gather x1 -> x0, waiting for transfers between devices: 40 us -> none  [shards(): own_cluster = lax.all_gather(unit_rows, 'rep', axis=0, tiled=True)]
    ppermute x12 -> x9, starting transfers between devices: 49.7 us -> 32.7 us  [the longest x6 24 us: over_cluster(): lax.ppermute(block, 'cluster', [(source(i) % n, i) for i in range(n)])]
    pmax x1 -> x0, blocking collectives: 9.32 us -> none  [shards(): column_best = lax.pmax(jnp.stack(column_list, axis=0), 'rep')]
    all_to_all x0 -> x1, starting transfers between devices: none -> 6.76 us  [shards(): row_best = jnp.max(lax.all_to_all(best, 'rep', 0, 0), axis=0)]
    pallas_call x0 -> x2, Pallas kernels: none -> 6.55 us  [the longest x1 4.12 us: shards(): pl.pallas_call(maxima_kernel, out_shape=jax.ShapeDtypeStruct((4, rows), j...]
    dot_general x2 -> x0, matrix products: 5.46 us -> none  [score_tile(): lax.dot_general(unit_rows, partner_rows, (((1,), (1,)), ((), ())), prefer...]
    all_to_all x0 -> x1, waiting for transfers between devices: none -> 3.84 us  [shards(): row_best = jnp.max(lax.all_to_all(best, 'rep', 0, 0), axis=0)]
  transfers between devices with their start and end apart: 13 -> 10, of which waited for: 9 -> 4; matrix products, arithmetic and copies ran while one was open for 3% -> 0% of each run, Pallas kernels for 0% -> 0%
where the time goes in v1:
time: 86.2 us; the launch traced here: 85.4 us
  starting transfers between devices  39.5 us (46%)
  waiting for transfers between devices  35.1 us (41%)
  Pallas kernels  6.55 us (8%)
  local copies, waits for them, and re-layouts  2.92 us (3%)
    ppermute x3, waiting for transfers between devices, over_rep(): return lax.ppermute(block, 'rep', [((i + away) % n, i) for i in range(n)])  31.3 us
    ppermute x6, starting transfers between devices, over_cluster(): lax.ppermute(block, 'cluster', [(source(i) % n, i) for i in range(n)])  24 us
    ppermute x3, starting transfers between devices, over_rep(): return lax.ppermute(block, 'rep', [((i + away) % n, i) for i in range(n)])  8.68 us
    all_to_all x1, starting transfers between devices, shards(): row_best = jnp.max(lax.all_to_all(best, 'rep', 0, 0), axis=0)  6.76 us
    pallas_call x1, Pallas kernels, shards(): pl.pallas_call(maxima_kernel, out_shape=jax.ShapeDtypeStruct((4, rows), j...  4.12 us
    all_to_all x1, waiting for transfers between devices, shards(): row_best = jnp.max(lax.all_to_all(best, 'rep', 0, 0), axis=0)  3.84 us
    pallas_call x1, Pallas kernels, shards(): pl.pallas_call(norm_kernel, out_shape=(jax.ShapeDtypeStruct((rows, width)...  2.42 us
    unnamed x5, local copies, waits for them, and re-layouts  2.33 us
  transfers between devices with their start and end apart: 10, of which 4 were waited for; matrix products, arithmetic and copies ran while one was open for 0% of the time, Pallas kernels for 0%

profile of v1, /device:TPU:2, one launch (start us, length us, event | category | flops | bytes accessed | tf_op | source)
XLA Modules:
  0.0 85.4 jit_solution(17890003871139361855)
XLA Ops:
  0.0 1.3 %copy.7.offset_ref = s32[2,1]{1,0:T(2,128)} copy(s32[2,1]{0,1:T(1,128)} %param.5) | data formatting | bytes 16 | tf_op args[2]
  1.9 2.4 %unit_rows.1 = (bf16[256,1024]{1,0:T(8,128)(2,1)}, bf16[272,1024]{1,0:T(8,128)(2,1)}) custom-call(s32[1]{0:T(128)} %copy.9.size_ref, s32[2,1]{1,0:T(2,128)} %copy.7.offset_ref, f32[256,1024]{1,0:T(8,128)} %rows_ref.1), custom_call_target="tpu_custom_call" | custom-call | tf_op jit(solution)/shard_map/unit_rows/pallas_call | solution.py:73
  4.4 14.0 %collective-permute-start.4 = (bf16[272,1024]{1,0:T(8,128)(2,1)}, bf16[272,1024]{1,0:T(8,128)(2,1)S(1)}, u32[]{:S(2)}, u32[]{:S(2)}) collective-permute-start(bf16[272,1024]{1,0:T(8,128)(2,1)} %get-tuple-element.8), channel_id=1, source_target_pairs={{8,0},{12,4},{16,8},{20,12},{24,16},{28,20},{32,24},{36,28},{40,32... | collective-permute-start | bytes 1671176 | tf_op jit(solution)/shard_map/ppermute | solution.py:63
  18.4 1.9 %collective-permute-start.5 = (bf16[272,1024]{1,0:T(8,128)(2,1)}, bf16[272,1024]{1,0:T(8,128)(2,1)S(1)}, u32[]{:S(2)}, u32[]{:S(2)}) collective-permute-start(bf16[272,1024]{1,0:T(8,128)(2,1)} %get-tuple-element.8), channel_id=1, source_target_pairs={{504,0},{508,4},{0,8},{4,12},{8,16},{12,20},{16,24},{20,28},{24,32... | collective-permute-start | bytes 1671176 | tf_op jit(solution)/shard_map/ppermute | solution.py:63
  20.3 2.4 %collective-permute-start = (bf16[256,1024]{1,0:T(8,128)(2,1)}, bf16[256,1024]{1,0:T(8,128)(2,1)S(1)}, u32[]{:S(2)}, u32[]{:S(2)}) collective-permute-start(bf16[256,1024]{1,0:T(8,128)(2,1)} %get-tuple-element.7.refs_0_), channel_id=1, source_target_pairs={{1,0},{2,1},{3,2},{0,3},{5,4},{6,5},{7,6},{4,7},{9,8},{10,9},{11,1... | collective-permute-start | bytes 1572872 | tf_op jit(solution)/shard_map/ppermute | solution.py:68
  22.7 4.3 %collective-permute-start.1 = (bf16[256,1024]{1,0:T(8,128)(2,1)}, bf16[256,1024]{1,0:T(8,128)(2,1)S(1)}, u32[]{:S(2)}, u32[]{:S(2)}) collective-permute-start(bf16[256,1024]{1,0:T(8,128)(2,1)} %get-tuple-element.7.refs_0_), channel_id=1, source_target_pairs={{2,0},{3,1},{0,2},{1,3},{6,4},{7,5},{4,6},{5,7},{10,8},{11,9},{8,1... | collective-permute-start | bytes 1572872 | tf_op jit(solution)/shard_map/ppermute | solution.py:68
  27.1 1.9 %collective-permute-start.3 = (bf16[272,1024]{1,0:T(8,128)(2,1)}, bf16[272,1024]{1,0:T(8,128)(2,1)S(1)}, u32[]{:S(2)}, u32[]{:S(2)}) collective-permute-start(bf16[272,1024]{1,0:T(8,128)(2,1)} %get-tuple-element.8), channel_id=1, source_target_pairs={{4,0},{0,4},{12,8},{8,12},{20,16},{16,20},{28,24},{24,28},{36,32},... | collective-permute-start | bytes 1671176 | tf_op jit(solution)/shard_map/ppermute | solution.py:63
  29.0 7.3 %collective-permute-done.refs_1_ = bf16[256,1024]{1,0:T(8,128)(2,1)S(1)} collective-permute-done((bf16[256,1024]{1,0:T(8,128)(2,1)}, bf16[256,1024]{1,0:T(8,128)(2,1)S(1)}, u32[]{:S(2)}, u32[]{:S(2)}) %collective-permute-start) | collective-permute-done | bytes 524320 | tf_op jit(solution)/shard_map/ppermute | solution.py:68
  36.3 1.9 %collective-permute-start.8 = (bf16[272,1024]{1,0:T(8,128)(2,1)}, bf16[272,1024]{1,0:T(8,128)(2,1)S(1)}, u32[]{:S(2)}, u32[]{:S(2)}) collective-permute-start(bf16[272,1024]{1,0:T(8,128)(2,1)} %get-tuple-element.8), channel_id=1, source_target_pairs={{500,0},{16,4},{508,8},{24,12},{4,16},{32,20},{12,24},{40,28},{20,... | collective-permute-start | bytes 1671176 | tf_op jit(solution)/shard_map/ppermute | solution.py:63
  38.2 0.0 collective-permute-done.4.refs_5_
  38.2 1.9 %collective-permute-start.6 = (bf16[272,1024]{1,0:T(8,128)(2,1)S(1)}, bf16[272,1024]{1,0:T(8,128)(2,1)S(1)}, u32[]{:S(2)}, u32[]{:S(2)}) collective-permute-start(bf16[272,1024]{1,0:T(8,128)(2,1)S(1)} %collective-permute-done.4.refs_5_), channel_id=1, source_target_pairs={{4,0},{0,4},{12,8},{8,12},{20,16},{16,20},{28,24},{24,28},{36,32},... | collective-permute-start | bytes 1671176 | tf_op jit(solution)/shard_map/ppermute | solution.py:63
  40.2 0.0 collective-permute-done.5.refs_6_
  40.2 2.4 %collective-permute-start.7 = (bf16[272,1024]{1,0:T(8,128)(2,1)S(1)}, bf16[272,1024]{1,0:T(8,128)(2,1)S(1)}, u32[]{:S(2)}, u32[]{:S(2)}) collective-permute-start(bf16[272,1024]{1,0:T(8,128)(2,1)S(1)} %collective-permute-done.5.refs_6_), channel_id=1, source_target_pairs={{4,0},{0,4},{12,8},{8,12},{20,16},{16,20},{28,24},{24,28},{36,32},... | collective-permute-start | bytes 1671176 | tf_op jit(solution)/shard_map/ppermute | solution.py:63
  42.6 5.3 %collective-permute-done.1.refs_2_ = bf16[256,1024]{1,0:T(8,128)(2,1)S(1)} collective-permute-done((bf16[256,1024]{1,0:T(8,128)(2,1)}, bf16[256,1024]{1,0:T(8,128)(2,1)S(1)}, u32[]{:S(2)}, u32[]{:S(2)}) %collective-permute-start.1) | collective-permute-done | bytes 524320 | tf_op jit(solution)/shard_map/ppermute | solution.py:68
  47.9 1.9 %collective-permute-start.2 = (bf16[256,1024]{1,0:T(8,128)(2,1)}, bf16[256,1024]{1,0:T(8,128)(2,1)S(1)}, u32[]{:S(2)}, u32[]{:S(2)}) collective-permute-start(bf16[256,1024]{1,0:T(8,128)(2,1)} %get-tuple-element.7.refs_0_), channel_id=1, source_target_pairs={{3,0},{0,1},{1,2},{2,3},{7,4},{4,5},{5,6},{6,7},{11,8},{8,9},{9,10... | collective-permute-start | bytes 1572872 | tf_op jit(solution)/shard_map/ppermute | solution.py:68
  49.9 18.6 %collective-permute-done.2.refs_3_ = bf16[256,1024]{1,0:T(8,128)(2,1)S(1)} collective-permute-done((bf16[256,1024]{1,0:T(8,128)(2,1)}, bf16[256,1024]{1,0:T(8,128)(2,1)S(1)}, u32[]{:S(2)}, u32[]{:S(2)}) %collective-permute-start.2) | collective-permute-done | bytes 524320 | tf_op jit(solution)/shard_map/ppermute | solution.py:68
  68.5 0.0 collective-permute-done.6.refs_7_
  68.5 0.0 collective-permute-done.7.refs_8_
  68.5 1.0 %copy-done = bf16[256,1024]{1,0:T(8,128)(2,1)S(1)} copy-done((bf16[256,1024]{1,0:T(8,128)(2,1)S(1)}, bf16[256,1024]{1,0:T(8,128)(2,1)}, u32[]{:S(2)}) %copy-start) | copy-done | bytes 524312
  69.5 4.1 %maxima.1 = f32[4,256]{1,0:T(4,128)S(1)} custom-call(s32[2,1]{1,0:T(2,128)S(1)} %copy-done.1, bf16[256,1024]{1,0:T(8,128)(2,1)S(1)} %copy-done, bf16[256,1024]{1,0:T(8,128)(2,1)S(1)} %collective-permute-done.refs_1_, bf16[256,1024]{1,0:T(8,128)(2,1)S(1)} %collective-permute-done.1.refs_2_, bf16[256,1024]{1,0:T(8,128)(2,1)S(1)} %collective-permute-done.2.refs_3_, ...), custom_call_target="tpu_custom_call" | custom-call | tf_op jit(solution)/shard_map/maxima/pallas_call | solution.py:90
  73.7 0.6 copy.8
  74.3 6.8 %all-to-all-start = ((f32[4,1,256]{2,1,0:T(1,128)}), f32[4,1,256]{2,1,0:T(1,128)S(1)}, u32[]{:S(2)}, u32[]{:S(2)}) async-start(f32[4,1,256]{2,1,0:T(1,128)} %copy.8), calls=%async_computation | async-start | bytes 8192 | tf_op jit(solution)/shard_map/all_to_all | solution.py:98
  81.0 3.8 %all-to-all-done = f32[4,1,256]{2,1,0:T(1,128)S(1)} async-done(((f32[4,1,256]{2,1,0:T(1,128)}), f32[4,1,256]{2,1,0:T(1,128)S(1)}, u32[]{:S(2)}, u32[]{:S(2)}) %all-to-all-start) | async-done | bytes 4128 | tf_op jit(solution)/shard_map/all_to_all | solution.py:98
  84.9 0.6 compare_select_fusion
  (6 shorter events, 0.0 us)
Async XLA Ops:
  4.4 64.1 %copy-start.1 = (s32[2,1]{1,0:T(2,128)S(1)}, s32[2,1]{1,0:T(2,128)}, u32[]{:S(2)}) copy-start(s32[2,1]{1,0:T(2,128)} %copy.7.offset_ref) | copy-start | bytes 28
  4.4 33.8 %collective-permute-start.4 = (bf16[272,1024]{1,0:T(8,128)(2,1)}, bf16[272,1024]{1,0:T(8,128)(2,1)S(1)}, u32[]{:S(2)}, u32[]{:S(2)}) collective-permute-start(bf16[272,1024]{1,0:T(8,128)(2,1)} %get-tuple-element.8), channel_id=1, source_target_pairs={{8,0},{12,4},{16,8},{20,12},{24,16},{28,20},{32,24},{36,28},{40,32... | collective-permute-start | bytes 1671176 | tf_op jit(solution)/shard_map/ppermute | solution.py:63
  18.4 21.8 %collective-permute-start.5 = (bf16[272,1024]{1,0:T(8,128)(2,1)}, bf16[272,1024]{1,0:T(8,128)(2,1)S(1)}, u32[]{:S(2)}, u32[]{:S(2)}) collective-permute-start(bf16[272,1024]{1,0:T(8,128)(2,1)} %get-tuple-element.8), channel_id=1, source_target_pairs={{504,0},{508,4},{0,8},{4,12},{8,16},{12,20},{16,24},{20,28},{24,32... | collective-permute-start | bytes 1671176 | tf_op jit(solution)/shard_map/ppermute | solution.py:63
  20.3 16.0 %collective-permute-start = (bf16[256,1024]{1,0:T(8,128)(2,1)}, bf16[256,1024]{1,0:T(8,128)(2,1)S(1)}, u32[]{:S(2)}, u32[]{:S(2)}) collective-permute-start(bf16[256,1024]{1,0:T(8,128)(2,1)} %get-tuple-element.7.refs_0_), channel_id=1, source_target_pairs={{1,0},{2,1},{3,2},{0,3},{5,4},{6,5},{7,6},{4,7},{9,8},{10,9},{11,1... | collective-permute-start | bytes 1572872 | tf_op jit(solution)/shard_map/ppermute | solution.py:68
  22.7 25.2 %collective-permute-start.1 = (bf16[256,1024]{1,0:T(8,128)(2,1)}, bf16[256,1024]{1,0:T(8,128)(2,1)S(1)}, u32[]{:S(2)}, u32[]{:S(2)}) collective-permute-start(bf16[256,1024]{1,0:T(8,128)(2,1)} %get-tuple-element.7.refs_0_), channel_id=1, source_target_pairs={{2,0},{3,1},{0,2},{1,3},{6,4},{7,5},{4,6},{5,7},{10,8},{11,9},{8,1... | collective-permute-start | bytes 1572872 | tf_op jit(solution)/shard_map/ppermute | solution.py:68
  27.1 41.4 %collective-permute-start.3 = (bf16[272,1024]{1,0:T(8,128)(2,1)}, bf16[272,1024]{1,0:T(8,128)(2,1)S(1)}, u32[]{:S(2)}, u32[]{:S(2)}) collective-permute-start(bf16[272,1024]{1,0:T(8,128)(2,1)} %get-tuple-element.8), channel_id=1, source_target_pairs={{4,0},{0,4},{12,8},{8,12},{20,16},{16,20},{28,24},{24,28},{36,32},... | collective-permute-start | bytes 1671176 | tf_op jit(solution)/shard_map/ppermute | solution.py:63
  36.3 32.2 %collective-permute-start.8 = (bf16[272,1024]{1,0:T(8,128)(2,1)}, bf16[272,1024]{1,0:T(8,128)(2,1)S(1)}, u32[]{:S(2)}, u32[]{:S(2)}) collective-permute-start(bf16[272,1024]{1,0:T(8,128)(2,1)} %get-tuple-element.8), channel_id=1, source_target_pairs={{500,0},{16,4},{508,8},{24,12},{4,16},{32,20},{12,24},{40,28},{20,... | collective-permute-start | bytes 1671176 | tf_op jit(solution)/shard_map/ppermute | solution.py:63
  38.2 30.2 %collective-permute-start.6 = (bf16[272,1024]{1,0:T(8,128)(2,1)S(1)}, bf16[272,1024]{1,0:T(8,128)(2,1)S(1)}, u32[]{:S(2)}, u32[]{:S(2)}) collective-permute-start(bf16[272,1024]{1,0:T(8,128)(2,1)S(1)} %collective-permute-done.4.refs_5_), channel_id=1, source_target_pairs={{4,0},{0,4},{12,8},{8,12},{20,16},{16,20},{28,24},{24,28},{36,32},... | collective-permute-start | bytes 1671176 | tf_op jit(solution)/shard_map/ppermute | solution.py:63
  40.2 28.3 %collective-permute-start.7 = (bf16[272,1024]{1,0:T(8,128)(2,1)S(1)}, bf16[272,1024]{1,0:T(8,128)(2,1)S(1)}, u32[]{:S(2)}, u32[]{:S(2)}) collective-permute-start(bf16[272,1024]{1,0:T(8,128)(2,1)S(1)} %collective-permute-done.5.refs_6_), channel_id=1, source_target_pairs={{4,0},{0,4},{12,8},{8,12},{20,16},{16,20},{28,24},{24,28},{36,32},... | collective-permute-start | bytes 1671176 | tf_op jit(solution)/shard_map/ppermute | solution.py:63
  47.9 20.5 %collective-permute-start.2 = (bf16[256,1024]{1,0:T(8,128)(2,1)}, bf16[256,1024]{1,0:T(8,128)(2,1)S(1)}, u32[]{:S(2)}, u32[]{:S(2)}) collective-permute-start(bf16[256,1024]{1,0:T(8,128)(2,1)} %get-tuple-element.7.refs_0_), channel_id=1, source_target_pairs={{3,0},{0,1},{1,2},{2,3},{7,4},{4,5},{5,6},{6,7},{11,8},{8,9},{9,10... | collective-permute-start | bytes 1572872 | tf_op jit(solution)/shard_map/ppermute | solution.py:68
  68.5 1.0 %copy-start = (bf16[256,1024]{1,0:T(8,128)(2,1)S(1)}, bf16[256,1024]{1,0:T(8,128)(2,1)}, u32[]{:S(2)}) copy-start(bf16[256,1024]{1,0:T(8,128)(2,1)} %get-tuple-element.7.refs_0_) | copy-start | bytes 1572868
  74.3 10.6 %all-to-all-start = ((f32[4,1,256]{2,1,0:T(1,128)}), f32[4,1,256]{2,1,0:T(1,128)S(1)}, u32[]{:S(2)}, u32[]{:S(2)}) async-start(f32[4,1,256]{2,1,0:T(1,128)} %copy.8), calls=%async_computation | async-start | bytes 8192 | tf_op jit(solution)/shard_map/all_to_all | solution.py:98

commit v2 on v1

v2 whole, which is shorter than its diff:
```python
import jax
import jax.numpy as jnp
from jax import lax
from jax.experimental import pallas as pl
from jax.experimental.pallas import tpu as pltpu
from jax.sharding import PartitionSpec as P

META = 16
VMEM = pl.BlockSpec(memory_space=pltpu.VMEM)
SMEM = pl.BlockSpec(memory_space=pltpu.SMEM)
TAKEN = ((2, 2, 2, 2), (-1, -3, -1, -3), (1, 3, -3, -1))


def norm_kernel(size_ref, offset_ref, rows_ref, copies_ref, payload_ref):
    rows, width = rows_ref.shape
    values = rows_ref[...]
    norms = jnp.sqrt(jnp.sum(values * values, axis=1, keepdims=True) + 1e-06)
    unit = (values / norms).astype(jnp.bfloat16)
    for k in range(copies_ref.shape[0]):
        copies_ref[k] = unit
    payload_ref[0:rows, :] = unit
    used = jnp.clip(size_ref[0] - lax.axis_index("rep") * rows, 0, rows)
    line = lax.broadcasted_iota(jnp.int32, (META, width), 0)
    meta = jnp.where(line == 0, used, 0)
    for k in range(offset_ref.shape[1]):
        meta = jnp.where(line == k + 1, offset_ref[0, k], meta)
    payload_ref[rows:, :] = meta.astype(jnp.float32).astype(jnp.bfloat16)


def maxima_kernel(size_ref, offset_ref, own_ref, *refs):
    payloads, row_ref, column_refs = refs[:3], refs[3], refs[4:]
    reps, rows, _ = own_ref.shape
    place = lax.rem(lax.axis_index("cluster"), 4)
    best = [jnp.full((1, rows), -4.0, jnp.float32) for _ in range(reps)]
    lane = lax.broadcasted_iota(jnp.int32, (1, rows), 1)
    line = lax.broadcasted_iota(jnp.int32, (rows, 128), 0).astype(jnp.float32)
    for payload, column_ref, taken in zip(payloads, column_refs, TAKEN):
        delta = jnp.int32(taken[0])
        for k in range(1, 4):
            delta = jnp.where(place == k, taken[k], delta)
        meta = payload[rows:, 0:128].astype(jnp.float32)
        mine = jnp.float32(0.0)
        theirs = jnp.zeros((1, 128), jnp.float32)
        for k in range(offset_ref.shape[1]):
            mine = jnp.where(offset_ref[0, k] == delta, 1.0, mine)
            theirs = jnp.where(meta[k + 1 : k + 2, :] == (-delta).astype(jnp.float32), 1.0, theirs)
        paired = jnp.where(delta > 0, mine, theirs)
        row_bias = jnp.where(line < meta[0:1, :] * paired, 0.0, -8.0)
        row_bias = jnp.concatenate([row_bias] * (rows // 128), axis=1)
        found = jnp.full((rows, 128), -4.0, jnp.float32)
        for k in range(reps):
            scores = lax.dot_general(
                payload[0:rows, :], own_ref[k], (((1,), (1,)), ((), ())), preferred_element_type=jnp.float32
            )
            best[k] = jnp.maximum(best[k], jnp.max(scores + row_bias, axis=0, keepdims=True))
            lane_bias = jnp.where(lane + k * rows < size_ref[0], 0.0, -8.0)
            scores = scores + lane_bias
            for piece in range(rows // 128):
                found = jnp.maximum(found, scores[:, piece * 128 : (piece + 1) * 128])
        column = jnp.max(found.T, axis=0, keepdims=True)
        flags = jnp.concatenate([paired] * (rows // 128), axis=1)
        column_ref[...] = jnp.where(flags > 0.5, column, -4.0)
    for k in range(reps):
        row_ref[k] = best[k]


def shifted(block, moves):
    n = lax.axis_size("cluster")
    return lax.ppermute(block, "cluster", [((i + moves[i % 4]) % n, i) for i in range(n)])


def returned(block, moves):
    n = lax.axis_size("cluster")
    return lax.ppermute(block, "cluster", [(i, (i + moves[i % 4]) % n) for i in range(n)])


def shards(embeddings, cluster_sizes, offsets):
    rows, width = embeddings.shape
    reps = lax.axis_size("rep")
    flat_offsets = offsets.T
    copies, payload = pl.pallas_call(
        norm_kernel,
        out_shape=(
            jax.ShapeDtypeStruct((reps, rows, width), jnp.bfloat16),
            jax.ShapeDtypeStruct((rows + META, width), jnp.bfloat16),
        ),
        in_specs=[SMEM, SMEM, VMEM],
        out_specs=(VMEM, VMEM),
        name="unit_rows",
        compiler_params=pltpu.CompilerParams(vmem_limit_bytes=32 * 1024 * 1024),
    )(cluster_sizes, flat_offsets, embeddings)
    own = lax.all_to_all(copies, "rep", 0, 0, tiled=True)
    taken = [shifted(payload, moves) for moves in TAKEN]
    row_part, *column_parts = pl.pallas_call(
        maxima_kernel,
        out_shape=(jax.ShapeDtypeStruct((reps, 1, rows), jnp.float32),)
        + (jax.ShapeDtypeStruct((1, rows), jnp.float32),) * 3,
        in_specs=[SMEM, SMEM] + [VMEM] * 4,
        out_specs=(VMEM,) * 4,
        name="maxima",
        compiler_params=pltpu.CompilerParams(vmem_limit_bytes=32 * 1024 * 1024),
    )(cluster_sizes, flat_offsets, own, *taken)
    row_best = jnp.max(lax.all_to_all(row_part, "rep", 0, 0, tiled=True), axis=0)
    for part, moves in zip(column_parts, TAKEN):
        row_best = jnp.maximum(row_best, returned(part, moves))
    row_ids = lax.axis_index("rep") * rows + jnp.arange(rows, dtype=jnp.int32)
    return jnp.where(row_ids < cluster_sizes[0], row_best[0], 0.0)


def solution(mesh):
    return jax.shard_map(
        shards,
        mesh=mesh,
        in_specs=(P(("cluster", "rep"), None), P("cluster"), P(None, "cluster")),
        out_specs=P(("cluster", "rep")),
        check_vma=False,
    )
```

time: 86.2 us -> 72.9 us (0.85)
  waiting for transfers between devices: 35.1 us -> 18.2 us
  starting transfers between devices: 39.5 us -> 43.1 us
  local copies, waits for them, and re-layouts: 2.92 us -> 5.09 us
  Pallas kernels: 6.55 us -> 4.7 us
    ppermute x9 -> x6, waiting for transfers between devices: 31.3 us -> 18.2 us  [the longest x3 13.2 us: shifted(): lax.ppermute(block, 'cluster', [((i + moves[i % 4]) % n, i) for i in rang...]
    all_to_all x1 -> x2, starting transfers between devices: 6.76 us -> 14.4 us  [the longest x1 9.61 us: shards(): own = lax.all_to_all(copies, 'rep', 0, 0, tiled=True)]
    ppermute x9 -> x6, starting transfers between devices: 32.7 us -> 28.7 us  [the longest x3 15.5 us: shifted(): lax.ppermute(block, 'cluster', [((i + moves[i % 4]) % n, i) for i in rang...]
    all_to_all x1 -> x2, waiting for transfers between devices: 3.84 us -> 0.01 us  [the longest x1 0.01 us: shards(): own = lax.all_to_all(copies, 'rep', 0, 0, tiled=True)]
    unnamed x5 -> x12, local copies, waits for them, and re-layouts: 2.33 us -> 5.09 us
    pallas_call x2, Pallas kernels: 6.55 us -> 4.7 us  [the longest x1 3.06 us: shards(): pl.pallas_call(maxima_kernel, out_shape=(jax.ShapeDtypeStruct((reps, 1, r...]
  transfers between devices with their start and end apart: 10 -> 8, of which waited for: 4 -> 3; matrix products, arithmetic and copies ran while one was open for 0% -> 0% of each run, Pallas kernels for 0% -> 0%
where the time goes in v2:
time: 72.9 us; the launch traced here: 72.4 us
  starting transfers between devices  43.1 us (59%)
  waiting for transfers between devices  18.2 us (25%)
  local copies, waits for them, and re-layouts  5.09 us (7%)
  Pallas kernels  4.7 us (6%)
  between operations  0.75 us (1%)
    ppermute x3, starting transfers between devices, shifted(): lax.ppermute(block, 'cluster', [((i + moves[i % 4]) % n, i) for i in rang...  15.5 us
    ppermute x3, waiting for transfers between devices, shifted(): lax.ppermute(block, 'cluster', [((i + moves[i % 4]) % n, i) for i in rang...  13.2 us
    ppermute x3, starting transfers between devices, returned(): lax.ppermute(block, 'cluster', [(i, (i + moves[i % 4]) % n) for i in rang...  13.2 us
    all_to_all x1, starting transfers between devices, shards(): own = lax.all_to_all(copies, 'rep', 0, 0, tiled=True)  9.61 us
    unnamed x12, local copies, waits for them, and re-layouts  5.09 us
    ppermute x3, waiting for transfers between devices, returned(): lax.ppermute(block, 'cluster', [(i, (i + moves[i % 4]) % n) for i in rang...  4.99 us
    all_to_all x1, starting transfers between devices, shards(): lax.all_to_all(row_part, 'rep', 0, 0, tiled=True)  4.8 us
    pallas_call x1, Pallas kernels, shards(): pl.pallas_call(maxima_kernel, out_shape=(jax.ShapeDtypeStruct((reps, 1, r...  3.06 us
  transfers between devices with their start and end apart: 8, of which 3 were waited for; matrix products, arithmetic and copies ran while one was open for 0% of the time, Pallas kernels for 0%

profile of v2, /device:TPU:2, one launch (start us, length us, event | category | flops | bytes accessed | tf_op | source)
XLA Modules:
  0.0 72.4 jit_solution(533051594992340388)
XLA Ops:
  0.7 1.2 %copy-done.1 = f32[256,1024]{1,0:T(8,128)S(1)} copy-done((f32[256,1024]{1,0:T(8,128)S(1)}, f32[256,1024]{1,0:T(8,128)}, u32[]{:S(2)}) %copy-start.1) | copy-done | bytes 1048600
  1.9 0.7 copy-done.4
  2.5 1.6 %unit_rows.1 = (bf16[4,256,1024]{2,1,0:T(8,128)(2,1)S(1)}, bf16[272,1024]{1,0:T(8,128)(2,1)}) custom-call(s32[1]{0:T(128)} %copy.4.size_ref, s32[1,2]{1,0:T(1,128)S(1)} %bitcast.5, f32[256,1024]{1,0:T(8,128)S(1)} %copy-done.1), custom_call_target="tpu_custom_call" | custom-call | tf_op jit(solution)/shard_map/unit_rows/pallas_call | solution.py:81
  4.2 1.3 %copy-done = bf16[4,256,1024]{2,1,0:T(8,128)(2,1)} copy-done((bf16[4,256,1024]{2,1,0:T(8,128)(2,1)}, bf16[4,256,1024]{2,1,0:T(8,128)(2,1)S(1)}, u32[]{:S(2)}) %copy-start) | copy-done | bytes 2097176
  5.5 9.6 %all-to-all-start = ((bf16[4,256,1024]{2,1,0:T(8,128)(2,1)}), bf16[4,256,1024]{2,1,0:T(8,128)(2,1)S(1)}, u32[]{:S(2)}, u32[]{:S(2)}) async-start(bf16[4,256,1024]{2,1,0:T(8,128)(2,1)} %copy-done), calls=%async_computation | async-start | bytes 4194304 | tf_op jit(solution)/shard_map/all_to_all | solution.py:92
  15.1 9.2 %collective-permute-start = (bf16[272,1024]{1,0:T(8,128)(2,1)}, bf16[272,1024]{1,0:T(8,128)(2,1)S(1)}, u32[]{:S(2)}, u32[]{:S(2)}) collective-permute-start(bf16[272,1024]{1,0:T(8,128)(2,1)} %get-tuple-element.12), channel_id=1, source_target_pairs={{8,0},{12,4},{16,8},{20,12},{24,16},{28,20},{32,24},{36,28},{40,32... | collective-permute-start | bytes 1671176 | tf_op jit(solution)/shard_map/ppermute | solution.py:69
  24.3 1.9 %collective-permute-start.1 = (bf16[272,1024]{1,0:T(8,128)(2,1)}, bf16[272,1024]{1,0:T(8,128)(2,1)S(1)}, u32[]{:S(2)}, u32[]{:S(2)}) collective-permute-start(bf16[272,1024]{1,0:T(8,128)(2,1)} %get-tuple-element.12), channel_id=1, source_target_pairs={{508,0},{504,4},{4,8},{0,12},{12,16},{8,20},{20,24},{16,28},{28,32... | collective-permute-start | bytes 1671176 | tf_op jit(solution)/shard_map/ppermute | solution.py:69
  26.2 4.4 %collective-permute-start.2 = (bf16[272,1024]{1,0:T(8,128)(2,1)}, bf16[272,1024]{1,0:T(8,128)(2,1)S(1)}, u32[]{:S(2)}, u32[]{:S(2)}) collective-permute-start(bf16[272,1024]{1,0:T(8,128)(2,1)} %get-tuple-element.12), channel_id=1, source_target_pairs={{4,0},{16,4},{508,8},{8,12},{20,16},{32,20},{12,24},{24,28},{36,32... | collective-permute-start | bytes 1671176 | tf_op jit(solution)/shard_map/ppermute | solution.py:69
  30.7 5.3 %collective-permute-done.refs_0_ = bf16[272,1024]{1,0:T(8,128)(2,1)S(1)} collective-permute-done((bf16[272,1024]{1,0:T(8,128)(2,1)}, bf16[272,1024]{1,0:T(8,128)(2,1)S(1)}, u32[]{:S(2)}, u32[]{:S(2)}) %collective-permute-start) | collective-permute-done | bytes 557088 | tf_op jit(solution)/shard_map/ppermute | solution.py:69
  35.9 7.9 %collective-permute-done.1.refs_1_ = bf16[272,1024]{1,0:T(8,128)(2,1)S(1)} collective-permute-done((bf16[272,1024]{1,0:T(8,128)(2,1)}, bf16[272,1024]{1,0:T(8,128)(2,1)S(1)}, u32[]{:S(2)}, u32[]{:S(2)}) %collective-permute-start.1) | collective-permute-done | bytes 557088 | tf_op jit(solution)/shard_map/ppermute | solution.py:69
  43.8 0.0 collective-permute-done.2.refs_2_
  43.8 0.8 %copy-done.2 = bf16[272,1024]{1,0:T(8,128)(2,1)} copy-done((bf16[272,1024]{1,0:T(8,128)(2,1)}, bf16[272,1024]{1,0:T(8,128)(2,1)S(1)}, u32[]{:S(2)}) %copy-start.2) | copy-done | bytes 557080
  44.7 0.0 all-to-all-done.own_ref
  44.7 1.1 %copy-done.3 = bf16[272,1024]{1,0:T(8,128)(2,1)S(1)} copy-done((bf16[272,1024]{1,0:T(8,128)(2,1)S(1)}, bf16[272,1024]{1,0:T(8,128)(2,1)}, u32[]{:S(2)}) %copy-start.3) | copy-done | bytes 557080
  45.7 3.1 %maxima.1 = (f32[4,1,256]{2,1,0:T(1,128)}, f32[1,256]{1,0:T(1,128)S(1)}, f32[1,256]{1,0:T(1,128)S(1)}, f32[1,256]{1,0:T(1,128)S(1)}) custom-call(s32[1]{0:T(128)} %copy.4.size_ref, s32[1,2]{1,0:T(1,128)S(1)} %bitcast.6, bf16[4,256,1024]{2,1,0:T(8,128)(2,1)S(1)} %all-to-all-done.own_ref, bf16[272,1024]{1,0:T(8,128)(2,1)S(1)} %collective-permute-done.refs_0_, ...), custom_call_target="tpu_custom_call" | custom-call | tf_op jit(solution)/shard_map/maxima/pallas_call | solution.py:94
  48.8 4.8 %all-to-all-start.1 = ((f32[4,1,256]{2,1,0:T(1,128)}), f32[4,1,256]{2,1,0:T(1,128)S(1)}, u32[]{:S(2)}, u32[]{:S(2)}) async-start(f32[4,1,256]{2,1,0:T(1,128)} %get-tuple-element.13), calls=%async_computation.1 | async-start | bytes 8192 | tf_op jit(solution)/shard_map/all_to_all | solution.py:103
  53.6 1.9 %collective-permute-start.5 = (f32[1,256]{1,0:T(1,128)S(1)}, f32[1,256]{1,0:T(1,128)S(1)}, u32[]{:S(2)}, u32[]{:S(2)}) collective-permute-start(f32[1,256]{1,0:T(1,128)S(1)} %get-tuple-element.16), channel_id=1, source_target_pairs={{0,4},{4,16},{8,508},{12,8},{16,20},{20,32},{24,12},{28,24},{32,36... | collective-permute-start | bytes 3080 | tf_op jit(solution)/shard_map/ppermute | solution.py:74
  55.5 7.5 %collective-permute-start.4 = (f32[1,256]{1,0:T(1,128)S(1)}, f32[1,256]{1,0:T(1,128)S(1)}, u32[]{:S(2)}, u32[]{:S(2)}) collective-permute-start(f32[1,256]{1,0:T(1,128)S(1)} %get-tuple-element.15), channel_id=1, source_target_pairs={{0,508},{4,504},{8,4},{12,0},{16,12},{20,8},{24,20},{28,16},{32,28... | collective-permute-start | bytes 3080 | tf_op jit(solution)/shard_map/ppermute | solution.py:74
  63.0 3.7 %collective-permute-start.3 = (f32[1,256]{1,0:T(1,128)S(1)}, f32[1,256]{1,0:T(1,128)S(1)}, u32[]{:S(2)}, u32[]{:S(2)}) collective-permute-start(f32[1,256]{1,0:T(1,128)S(1)} %get-tuple-element.14), channel_id=1, source_target_pairs={{0,8},{4,12},{8,16},{12,20},{16,24},{20,28},{24,32},{28,36},{32,40... | collective-permute-start | bytes 3080 | tf_op jit(solution)/shard_map/ppermute | solution.py:74
  66.8 0.0 all-to-all-done.1
  66.8 0.0 collective-permute-done.5
  66.8 0.0 collective-permute-done.4
  66.8 5.0 %collective-permute-done.3 = f32[1,256]{1,0:T(1,128)S(1)} collective-permute-done((f32[1,256]{1,0:T(1,128)S(1)}, f32[1,256]{1,0:T(1,128)S(1)}, u32[]{:S(2)}, u32[]{:S(2)}) %collective-permute-start.3) | collective-permute-done | bytes 1056 | tf_op jit(solution)/shard_map/ppermute | solution.py:74
  71.8 0.6 compare_select_fusion
  (9 shorter events, 0.0 us)
Async XLA Ops:
  0.7 1.2 %copy-start.1 = (f32[256,1024]{1,0:T(8,128)S(1)}, f32[256,1024]{1,0:T(8,128)}, u32[]{:S(2)}) copy-start(f32[256,1024]{1,0:T(8,128)} %rows_ref.1) | copy-start | bytes 3145732
  1.9 0.7 copy-start.4
  4.2 1.3 %copy-start = (bf16[4,256,1024]{2,1,0:T(8,128)(2,1)}, bf16[4,256,1024]{2,1,0:T(8,128)(2,1)S(1)}, u32[]{:S(2)}) copy-start(bf16[4,256,1024]{2,1,0:T(8,128)(2,1)S(1)} %get-tuple-element.11) | copy-start | bytes 6291460
  5.5 39.2 %copy-start.5 = (s32[2,1]{0,1:T(1,128)S(1)}, s32[2,1]{0,1:T(1,128)}, u32[]{:S(2)}) copy-start(s32[2,1]{0,1:T(1,128)} %param.5) | copy-start | bytes 28
  5.5 39.2 %all-to-all-start = ((bf16[4,256,1024]{2,1,0:T(8,128)(2,1)}), bf16[4,256,1024]{2,1,0:T(8,128)(2,1)S(1)}, u32[]{:S(2)}, u32[]{:S(2)}) async-start(bf16[4,256,1024]{2,1,0:T(8,128)(2,1)} %copy-done), calls=%async_computation | async-start | bytes 4194304 | tf_op jit(solution)/shard_map/all_to_all | solution.py:92
  15.1 20.8 %collective-permute-start = (bf16[272,1024]{1,0:T(8,128)(2,1)}, bf16[272,1024]{1,0:T(8,128)(2,1)S(1)}, u32[]{:S(2)}, u32[]{:S(2)}) collective-permute-start(bf16[272,1024]{1,0:T(8,128)(2,1)} %get-tuple-element.12), channel_id=1, source_target_pairs={{8,0},{12,4},{16,8},{20,12},{24,16},{28,20},{32,24},{36,28},{40,32... | collective-permute-start | bytes 1671176 | tf_op jit(solution)/shard_map/ppermute | solution.py:69
  24.3 19.5 %collective-permute-start.1 = (bf16[272,1024]{1,0:T(8,128)(2,1)}, bf16[272,1024]{1,0:T(8,128)(2,1)S(1)}, u32[]{:S(2)}, u32[]{:S(2)}) collective-permute-start(bf16[272,1024]{1,0:T(8,128)(2,1)} %get-tuple-element.12), channel_id=1, source_target_pairs={{508,0},{504,4},{4,8},{0,12},{12,16},{8,20},{20,24},{16,28},{28,32... | collective-permute-start | bytes 1671176 | tf_op jit(solution)/shard_map/ppermute | solution.py:69
  26.2 17.6 %collective-permute-start.2 = (bf16[272,1024]{1,0:T(8,128)(2,1)}, bf16[272,1024]{1,0:T(8,128)(2,1)S(1)}, u32[]{:S(2)}, u32[]{:S(2)}) collective-permute-start(bf16[272,1024]{1,0:T(8,128)(2,1)} %get-tuple-element.12), channel_id=1, source_target_pairs={{4,0},{16,4},{508,8},{8,12},{20,16},{32,20},{12,24},{24,28},{36,32... | collective-permute-start | bytes 1671176 | tf_op jit(solution)/shard_map/ppermute | solution.py:69
  43.8 0.8 %copy-start.2 = (bf16[272,1024]{1,0:T(8,128)(2,1)}, bf16[272,1024]{1,0:T(8,128)(2,1)S(1)}, u32[]{:S(2)}) copy-start(bf16[272,1024]{1,0:T(8,128)(2,1)S(1)} %collective-permute-done.2.refs_2_) | copy-start | bytes 1671172
  44.7 1.1 %copy-start.3 = (bf16[272,1024]{1,0:T(8,128)(2,1)S(1)}, bf16[272,1024]{1,0:T(8,128)(2,1)}, u32[]{:S(2)}) copy-start(bf16[272,1024]{1,0:T(8,128)(2,1)} %copy-done.2) | copy-start | bytes 1671172
  48.8 18.0 %all-to-all-start.1 = ((f32[4,1,256]{2,1,0:T(1,128)}), f32[4,1,256]{2,1,0:T(1,128)S(1)}, u32[]{:S(2)}, u32[]{:S(2)}) async-start(f32[4,1,256]{2,1,0:T(1,128)} %get-tuple-element.13), calls=%async_computation.1 | async-start | bytes 8192 | tf_op jit(solution)/shard_map/all_to_all | solution.py:103
  53.6 13.2 %collective-permute-start.5 = (f32[1,256]{1,0:T(1,128)S(1)}, f32[1,256]{1,0:T(1,128)S(1)}, u32[]{:S(2)}, u32[]{:S(2)}) collective-permute-start(f32[1,256]{1,0:T(1,128)S(1)} %get-tuple-element.16), channel_id=1, source_target_pairs={{0,4},{4,16},{8,508},{12,8},{16,20},{20,32},{24,12},{28,24},{32,36... | collective-permute-start | bytes 3080 | tf_op jit(solution)/shard_map/ppermute | solution.py:74
  55.5 11.3 %collective-permute-start.4 = (f32[1,256]{1,0:T(1,128)S(1)}, f32[1,256]{1,0:T(1,128)S(1)}, u32[]{:S(2)}, u32[]{:S(2)}) collective-permute-start(f32[1,256]{1,0:T(1,128)S(1)} %get-tuple-element.15), channel_id=1, source_target_pairs={{0,508},{4,504},{8,4},{12,0},{16,12},{20,8},{24,20},{28,16},{32,28... | collective-permute-start | bytes 3080 | tf_op jit(solution)/shard_map/ppermute | solution.py:74
  63.0 8.8 %collective-permute-start.3 = (f32[1,256]{1,0:T(1,128)S(1)}, f32[1,256]{1,0:T(1,128)S(1)}, u32[]{:S(2)}, u32[]{:S(2)}) collective-permute-start(f32[1,256]{1,0:T(1,128)S(1)} %get-tuple-element.14), channel_id=1, source_target_pairs={{0,8},{4,12},{8,16},{12,20},{16,24},{20,28},{24,32},{28,36},{32,40... | collective-permute-start | bytes 3080 | tf_op jit(solution)/shard_map/ppermute | solution.py:74

commit v3 on v1

v3 whole, which is shorter than its diff:
```python
import jax
import jax.numpy as jnp
from jax import lax
from jax.experimental import pallas as pl
from jax.experimental.pallas import tpu as pltpu
from jax.sharding import PartitionSpec as P

META = 16
CHUNKS = 4
VMEM = pl.BlockSpec(memory_space=pltpu.VMEM)
SMEM = pl.BlockSpec(memory_space=pltpu.SMEM)
HBM = pl.BlockSpec(memory_space=pltpu.HBM)
WIDE = pltpu.CompilerParams(vmem_limit_bytes=60 * 1024 * 1024)
SMALL = pltpu.CompilerParams(vmem_limit_bytes=12 * 1024 * 1024)


def norm_kernel(size_ref, offset_ref, rows_ref, copies_ref, payload_ref, size, offset, raw, unit, in_sems, out_sems):
    reps, rows, width = copies_ref.shape
    step = rows // CHUNKS
    loads = [
        pltpu.make_async_copy(rows_ref.at[pl.ds(c * step, step)], raw.at[pl.ds(c * step, step)], in_sems.at[c])
        for c in range(CHUNKS)
    ]
    loads.append(pltpu.make_async_copy(size_ref, size, in_sems.at[CHUNKS]))
    loads.append(pltpu.make_async_copy(offset_ref, offset, in_sems.at[CHUNKS + 1]))
    for load in loads:
        load.start()
    stores = []

    def store(source, target):
        copy = pltpu.make_async_copy(source, target, out_sems.at[len(stores)])
        copy.start()
        stores.append(copy)

    for c in range(CHUNKS):
        part = pl.ds(c * step, step)
        loads[c].wait()
        values = raw[part, :]
        norms = jnp.sqrt(jnp.sum(values * values, axis=1, keepdims=True) + 1e-06)
        unit[part, :] = (values * (1.0 / norms)).astype(jnp.bfloat16)
        for k in range(reps):
            store(unit.at[part], copies_ref.at[k, part])
        store(unit.at[part], payload_ref.at[part])
    loads[CHUNKS].wait()
    loads[CHUNKS + 1].wait()
    used = jnp.clip(size[0, 0] - lax.axis_index("rep") * rows, 0, rows)
    line = lax.broadcasted_iota(jnp.int32, (META, width), 0)
    meta = jnp.where(line == 0, used, 0)
    for k in range(offset_ref.shape[1]):
        meta = jnp.where(line == k + 1, offset[0, k], meta)
    unit[rows:, :] = meta.astype(jnp.float32).astype(jnp.bfloat16)
    store(unit.at[pl.ds(rows, META)], payload_ref.at[pl.ds(rows, META)])
    for copy in stores:
        copy.wait()


def row_bias(offset_ref, payload, delta, rows):
    meta = payload[rows : rows + META, 0:128].astype(jnp.float32)
    mine = jnp.float32(0.0)
    theirs = jnp.zeros((1, 128), jnp.float32)
    for k in range(offset_ref.shape[1]):
        mine = jnp.where(offset_ref[0, k] == delta, 1.0, mine)
        theirs = jnp.where(meta[k + 1 : k + 2, :] == (-delta).astype(jnp.float32), 1.0, theirs)
    paired = jnp.where(delta > 0, mine, theirs)
    line = lax.broadcasted_iota(jnp.int32, (rows, 128), 0).astype(jnp.float32)
    bias = jnp.where(line < meta[0:1, :] * paired, 0.0, -8.0)
    return jnp.concatenate([bias] * (rows // 128), axis=1)


def score(offset_ref, own_ref, payload, delta, best):
    reps, rows, _ = own_ref.shape
    bias = row_bias(offset_ref, payload, delta, rows)
    for k in range(reps):
        scores = lax.dot_general(
            payload[0:rows, :], own_ref[k], (((1,), (1,)), ((), ())), preferred_element_type=jnp.float32
        )
        best[k] = jnp.maximum(best[k], jnp.max(scores + bias, axis=0, keepdims=True))


def early_kernel(offset_ref, own_ref, ahead_ref, behind_ref, best_ref):
    reps, rows, _ = own_ref.shape
    best = [jnp.full((1, rows), -4.0, jnp.float32) for _ in range(reps)]
    score(offset_ref, own_ref, ahead_ref, jnp.int32(2), best)
    score(offset_ref, own_ref, behind_ref, jnp.int32(-2), best)
    for k in range(reps):
        best_ref[k] = best[k]


def late_kernel(
    offset_ref, own_ref, far_ref, mate_ref, ahead_ref, behind_ref, early_ref, best_ref, ahead, behind, sems
):
    reps, rows, _ = own_ref.shape
    odd = lax.rem(lax.axis_index("cluster"), 2)
    loads = [
        pltpu.make_async_copy(ahead_ref, ahead, sems.at[0]),
        pltpu.make_async_copy(behind_ref, behind, sems.at[1]),
    ]
    for load in loads:
        load.start()
    best = [early_ref[k] for k in range(reps)]
    score(offset_ref, own_ref, far_ref, 6 * odd - 3, best)
    score(offset_ref, own_ref, mate_ref, 1 - 2 * odd, best)
    loads[0].wait()
    score(offset_ref, own_ref, ahead, 3 - 2 * odd, best)
    loads[1].wait()
    score(offset_ref, own_ref, behind, -1 - 2 * odd, best)
    for k in range(reps):
        best_ref[k] = best[k]


def over_cluster(block, even, odd):
    n = lax.axis_size("cluster")
    return lax.ppermute(block, "cluster", [((i + (odd if i % 2 else even)) % n, i) for i in range(n)])


def shards(embeddings, cluster_sizes, offsets):
    rows, width = embeddings.shape
    reps = lax.axis_size("rep")
    flat_offsets = offsets.T
    flat_sizes = cluster_sizes.reshape(1, 1)
    payload_shape = jax.ShapeDtypeStruct((rows + META, width), jnp.bfloat16)
    copies, payload = pl.pallas_call(
        norm_kernel,
        out_shape=(jax.ShapeDtypeStruct((reps, rows, width), jnp.bfloat16), payload_shape),
        in_specs=[HBM, HBM, HBM],
        out_specs=(HBM, HBM),
        scratch_shapes=[
            pltpu.SMEM(flat_sizes.shape, jnp.int32),
            pltpu.SMEM(flat_offsets.shape, jnp.int32),
            pltpu.VMEM((rows, width), jnp.float32),
            pltpu.VMEM((rows + META, width), jnp.bfloat16),
            pltpu.SemaphoreType.DMA((CHUNKS + 2,)),
            pltpu.SemaphoreType.DMA((CHUNKS * (reps + 1) + 1,)),
        ],
        name="unit_rows",
        compiler_params=WIDE,
    )(flat_sizes, flat_offsets, embeddings)
    own = lax.all_to_all(copies, "rep", 0, 0, tiled=True)
    behind = over_cluster(payload, -2, -2)
    ahead = over_cluster(payload, 2, 2)
    mate = over_cluster(payload, 1, -1)
    far = over_cluster(payload, -3, 3)
    ahead_mate = over_cluster(ahead, 1, -1)
    behind_mate = over_cluster(behind, 1, -1)
    part_shape = jax.ShapeDtypeStruct((reps, 1, rows), jnp.float32)
    part = pl.pallas_call(
        early_kernel,
        out_shape=part_shape,
        in_specs=[SMEM] + [VMEM] * 3,
        out_specs=VMEM,
        name="early_maxima",
        compiler_params=SMALL,
    )(flat_offsets, own, ahead, behind)
    part = pl.pallas_call(
        late_kernel,
        out_shape=part_shape,
        in_specs=[SMEM] + [VMEM] * 3 + [HBM] * 2 + [VMEM],
        out_specs=VMEM,
        scratch_shapes=[
            pltpu.VMEM((rows + META, width), jnp.bfloat16),
            pltpu.VMEM((rows + META, width), jnp.bfloat16),
            pltpu.SemaphoreType.DMA((2,)),
        ],
        name="late_maxima",
        compiler_params=SMALL,
    )(flat_offsets, own, far, mate, ahead_mate, behind_mate, part)
    row_best = jnp.max(lax.all_to_all(part, "rep", 0, 0, tiled=True), axis=(0, 1))
    row_ids = lax.axis_index("rep") * rows + jnp.arange(rows, dtype=jnp.int32)
    return jnp.where(row_ids < cluster_sizes[0], row_best, 0.0)


def solution(mesh):
    return jax.shard_map(
        shards,
        mesh=mesh,
        in_specs=(P(("cluster", "rep"), None), P("cluster"), P(None, "cluster")),
        out_specs=P(("cluster", "rep")),
        check_vma=False,
    )
```

time: 86.2 us -> 61.3 us (0.71)
  waiting for transfers between devices: 35.1 us -> 14.3 us
  starting transfers between devices: 39.5 us -> 36 us
  local copies, waits for them, and re-layouts: 2.92 us -> 0.01 us
  Pallas kernels: 6.55 us -> 9.26 us
    ppermute x9 -> x6, waiting for transfers between devices: 31.3 us -> 10.4 us  [over_cluster(): lax.ppermute(block, 'cluster', [((i + (odd if i % 2 else even)) % n, i) f...]
    ppermute x9 -> x6, starting transfers between devices: 32.7 us -> 21.7 us  [over_cluster(): lax.ppermute(block, 'cluster', [((i + (odd if i % 2 else even)) % n, i) f...]
    all_to_all x1 -> x2, starting transfers between devices: 6.76 us -> 14.3 us  [the longest x1 9.49 us: shards(): own = lax.all_to_all(copies, 'rep', 0, 0, tiled=True)]
    pallas_call x2 -> x3, Pallas kernels: 6.55 us -> 9.26 us  [the longest x1 3.98 us: shards(): pl.pallas_call(late_kernel, out_shape=part_shape, in_specs=[SMEM] + [VMEM...]
    unnamed x5 -> x2, local copies, waits for them, and re-layouts: 2.33 us -> 0.01 us
    all_to_all x1 -> x2, waiting for transfers between devices: 3.84 us -> 3.84 us  [the longest x1 3.83 us: shards(): lax.all_to_all(part, 'rep', 0, 0, tiled=True)]
  transfers between devices with their start and end apart: 10 -> 8, of which waited for: 4 -> 4; matrix products, arithmetic and copies ran while one was open for 0% -> 0% of each run, Pallas kernels for 0% -> 4%
where the time goes in v3:
time: 61.3 us; the launch traced here: 60.8 us
  starting transfers between devices  36 us (59%)
  waiting for transfers between devices  14.3 us (23%)
  Pallas kernels  9.26 us (15%)
  between operations  0.76 us (1%)
    ppermute x6, starting transfers between devices, over_cluster(): lax.ppermute(block, 'cluster', [((i + (odd if i % 2 else even)) % n, i) f...  21.7 us
    ppermute x6, waiting for transfers between devices, over_cluster(): lax.ppermute(block, 'cluster', [((i + (odd if i % 2 else even)) % n, i) f...  10.4 us
    all_to_all x1, starting transfers between devices, shards(): own = lax.all_to_all(copies, 'rep', 0, 0, tiled=True)  9.49 us
    all_to_all x1, starting transfers between devices, shards(): lax.all_to_all(part, 'rep', 0, 0, tiled=True)  4.81 us
    pallas_call x1, Pallas kernels, shards(): pl.pallas_call(late_kernel, out_shape=part_shape, in_specs=[SMEM] + [VMEM...  3.98 us
    all_to_all x1, waiting for transfers between devices, shards(): lax.all_to_all(part, 'rep', 0, 0, tiled=True)  3.83 us
    pallas_call x1, Pallas kernels, shards(): pl.pallas_call(norm_kernel, out_shape=(jax.ShapeDtypeStruct((reps, rows,...  2.76 us
    pallas_call x1, Pallas kernels, shards(): pl.pallas_call(early_kernel, out_shape=part_shape, in_specs=[SMEM] + [VME...  2.53 us
  transfers between devices with their start and end apart: 8, of which 4 were waited for; matrix products, arithmetic and copies ran while one was open for 0% of the time, Pallas kernels for 4%

profile of v3, /device:TPU:2, one launch (start us, length us, event | category | flops | bytes accessed | tf_op | source)
XLA Modules:
  0.0 60.8 jit_solution(16791296848496990285)
XLA Ops:
  0.7 2.8 %unit_rows.1 = (bf16[4,256,1024]{2,1,0:T(8,128)(2,1)}, bf16[272,1024]{1,0:T(8,128)(2,1)}) custom-call(s32[1,1]{1,0:T(1,128)} %bitcast.4.size_ref, s32[1,2]{1,0:T(1,128)} %bitcast.5, f32[256,1024]{1,0:T(8,128)} %rows_ref.1), custom_call_target="tpu_custom_call" | custom-call | tf_op jit(solution)/shard_map/unit_rows/pallas_call | solution.py:122
  3.4 0.0 copy-start
  3.4 9.5 %all-to-all-start = ((bf16[4,256,1024]{2,1,0:T(8,128)(2,1)}), bf16[4,256,1024]{2,1,0:T(8,128)(2,1)S(1)}, u32[]{:S(2)}, u32[]{:S(2)}) async-start(bf16[4,256,1024]{2,1,0:T(8,128)(2,1)} %get-tuple-element.7), calls=%async_computation | async-start | bytes 4194304 | tf_op jit(solution)/shard_map/all_to_all | solution.py:138
  12.9 1.9 %collective-permute-start.4 = (bf16[272,1024]{1,0:T(8,128)(2,1)}, bf16[272,1024]{1,0:T(8,128)(2,1)}, u32[]{:S(2)}, u32[]{:S(2)}) collective-permute-start(bf16[272,1024]{1,0:T(8,128)(2,1)} %get-tuple-element.8), channel_id=1, source_target_pairs={{504,0},{508,4},{0,8},{4,12},{8,16},{12,20},{16,24},{20,28},{24,32... | collective-permute-start | bytes 1671176 | tf_op jit(solution)/shard_map/ppermute | solution.py:113
  14.8 9.2 %collective-permute-start.2 = (bf16[272,1024]{1,0:T(8,128)(2,1)}, bf16[272,1024]{1,0:T(8,128)(2,1)}, u32[]{:S(2)}, u32[]{:S(2)}) collective-permute-start(bf16[272,1024]{1,0:T(8,128)(2,1)} %get-tuple-element.8), channel_id=1, source_target_pairs={{8,0},{12,4},{16,8},{20,12},{24,16},{28,20},{32,24},{36,28},{40,32... | collective-permute-start | bytes 1671176 | tf_op jit(solution)/shard_map/ppermute | solution.py:113
  24.0 1.9 %collective-permute-start.1 = (bf16[272,1024]{1,0:T(8,128)(2,1)}, bf16[272,1024]{1,0:T(8,128)(2,1)S(1)}, u32[]{:S(2)}, u32[]{:S(2)}) collective-permute-start(bf16[272,1024]{1,0:T(8,128)(2,1)} %get-tuple-element.8), channel_id=1, source_target_pairs={{4,0},{0,4},{12,8},{8,12},{20,16},{16,20},{28,24},{24,28},{36,32},... | collective-permute-start | bytes 1671176 | tf_op jit(solution)/shard_map/ppermute | solution.py:113
  26.0 4.8 %collective-permute-start = (bf16[272,1024]{1,0:T(8,128)(2,1)}, bf16[272,1024]{1,0:T(8,128)(2,1)S(1)}, u32[]{:S(2)}, u32[]{:S(2)}) collective-permute-start(bf16[272,1024]{1,0:T(8,128)(2,1)} %get-tuple-element.8), channel_id=1, source_target_pairs={{500,0},{16,4},{508,8},{24,12},{4,16},{32,20},{12,24},{40,28},{20,... | collective-permute-start | bytes 1671176 | tf_op jit(solution)/shard_map/ppermute | solution.py:113
  30.8 5.4 %collective-permute-done.4.behind_ref = bf16[272,1024]{1,0:T(8,128)(2,1)} collective-permute-done((bf16[272,1024]{1,0:T(8,128)(2,1)}, bf16[272,1024]{1,0:T(8,128)(2,1)}, u32[]{:S(2)}, u32[]{:S(2)}) %collective-permute-start.4) | collective-permute-done | bytes 557088 | tf_op jit(solution)/shard_map/ppermute | solution.py:113
  36.2 1.9 %collective-permute-start.5 = (bf16[272,1024]{1,0:T(8,128)(2,1)}, bf16[272,1024]{1,0:T(8,128)(2,1)}, u32[]{:S(2)}, u32[]{:S(2)}) collective-permute-start(bf16[272,1024]{1,0:T(8,128)(2,1)} %collective-permute-done.4.behind_ref), channel_id=1, source_target_pairs={{4,0},{0,4},{12,8},{8,12},{20,16},{16,20},{28,24},{24,28},{36,32},... | collective-permute-start | bytes 1671176 | tf_op jit(solution)/shard_map/ppermute | solution.py:113
  38.1 0.9 %collective-permute-done.2.ahead_ref = bf16[272,1024]{1,0:T(8,128)(2,1)} collective-permute-done((bf16[272,1024]{1,0:T(8,128)(2,1)}, bf16[272,1024]{1,0:T(8,128)(2,1)}, u32[]{:S(2)}, u32[]{:S(2)}) %collective-permute-start.2) | collective-permute-done | bytes 557088 | tf_op jit(solution)/shard_map/ppermute | solution.py:113
  39.0 1.9 %collective-permute-start.3 = (bf16[272,1024]{1,0:T(8,128)(2,1)}, bf16[272,1024]{1,0:T(8,128)(2,1)}, u32[]{:S(2)}, u32[]{:S(2)}) collective-permute-start(bf16[272,1024]{1,0:T(8,128)(2,1)} %collective-permute-done.2.ahead_ref), channel_id=1, source_target_pairs={{4,0},{0,4},{12,8},{8,12},{20,16},{16,20},{28,24},{24,28},{36,32},... | collective-permute-start | bytes 1671176 | tf_op jit(solution)/shard_map/ppermute | solution.py:113
  41.0 0.0 all-to-all-done.own_ref
  41.0 0.0 copy-done
  41.0 2.5 %early_maxima.1.early_ref = f32[4,1,256]{2,1,0:T(1,128)S(1)} custom-call(s32[1,2]{1,0:T(1,128)S(1)} %bitcast.6, bf16[4,256,1024]{2,1,0:T(8,128)(2,1)S(1)} %all-to-all-done.own_ref, bf16[272,1024]{1,0:T(8,128)(2,1)} %collective-permute-done.2.ahead_ref, bf16[272,1024]{1,0:T(8,128)(2,1)} %collective-permute-done.4.behind_ref), custom_call_target="tpu_custom_call" | custom-call | tf_op jit(solution)/shard_map/early_maxima/pallas_call | solution.py:146
  43.5 0.0 collective-permute-done.1.mate_ref
  43.5 4.1 %collective-permute-done.far_ref = bf16[272,1024]{1,0:T(8,128)(2,1)S(1)} collective-permute-done((bf16[272,1024]{1,0:T(8,128)(2,1)}, bf16[272,1024]{1,0:T(8,128)(2,1)S(1)}, u32[]{:S(2)}, u32[]{:S(2)}) %collective-permute-start) | collective-permute-done | bytes 557088 | tf_op jit(solution)/shard_map/ppermute | solution.py:113
  47.6 0.0 collective-permute-done.5.behind_ref
  47.6 0.0 collective-permute-done.3.ahead_ref
  47.6 4.0 %late_maxima.1 = f32[4,1,256]{2,1,0:T(1,128)} custom-call(s32[1,2]{1,0:T(1,128)S(1)} %bitcast.7, bf16[4,256,1024]{2,1,0:T(8,128)(2,1)S(1)} %all-to-all-done.own_ref, bf16[272,1024]{1,0:T(8,128)(2,1)S(1)} %collective-permute-done.far_ref, bf16[272,1024]{1,0:T(8,128)(2,1)S(1)} %collective-permute-done.1.mate_ref, ...), custom_call_target="tpu_custom_call" | custom-call | tf_op jit(solution)/shard_map/late_maxima/pallas_call | solution.py:154
  51.6 4.8 %all-to-all-start.1 = ((f32[4,1,256]{2,1,0:T(1,128)}), f32[4,1,256]{2,1,0:T(1,128)S(1)}, u32[]{:S(2)}, u32[]{:S(2)}) async-start(f32[4,1,256]{2,1,0:T(1,128)} %late_maxima.1), calls=%async_computation.1 | async-start | bytes 8192 | tf_op jit(solution)/shard_map/all_to_all | solution.py:167
  56.4 3.8 %all-to-all-done.1 = f32[4,1,256]{2,1,0:T(1,128)S(1)} async-done(((f32[4,1,256]{2,1,0:T(1,128)}), f32[4,1,256]{2,1,0:T(1,128)S(1)}, u32[]{:S(2)}, u32[]{:S(2)}) %all-to-all-start.1) | async-done | bytes 4128 | tf_op jit(solution)/shard_map/all_to_all | solution.py:167
  60.3 0.6 compare_select_fusion
  (1 shorter events, 0.0 us)
Async XLA Ops:
  3.4 37.6 %copy-start = (s32[2,1]{0,1:T(1,128)S(1)}, s32[2,1]{0,1:T(1,128)}, u32[]{:S(2)}) copy-start(s32[2,1]{0,1:T(1,128)} %param.5) | copy-start | bytes 28
  3.4 37.5 %all-to-all-start = ((bf16[4,256,1024]{2,1,0:T(8,128)(2,1)}), bf16[4,256,1024]{2,1,0:T(8,128)(2,1)S(1)}, u32[]{:S(2)}, u32[]{:S(2)}) async-start(bf16[4,256,1024]{2,1,0:T(8,128)(2,1)} %get-tuple-element.7), calls=%async_computation | async-start | bytes 4194304 | tf_op jit(solution)/shard_map/all_to_all | solution.py:138
  12.9 23.3 %collective-permute-start.4 = (bf16[272,1024]{1,0:T(8,128)(2,1)}, bf16[272,1024]{1,0:T(8,128)(2,1)}, u32[]{:S(2)}, u32[]{:S(2)}) collective-permute-start(bf16[272,1024]{1,0:T(8,128)(2,1)} %get-tuple-element.8), channel_id=1, source_target_pairs={{504,0},{508,4},{0,8},{4,12},{8,16},{12,20},{16,24},{20,28},{24,32... | collective-permute-start | bytes 1671176 | tf_op jit(solution)/shard_map/ppermute | solution.py:113
  14.8 24.2 %collective-permute-start.2 = (bf16[272,1024]{1,0:T(8,128)(2,1)}, bf16[272,1024]{1,0:T(8,128)(2,1)}, u32[]{:S(2)}, u32[]{:S(2)}) collective-permute-start(bf16[272,1024]{1,0:T(8,128)(2,1)} %get-tuple-element.8), channel_id=1, source_target_pairs={{8,0},{12,4},{16,8},{20,12},{24,16},{28,20},{32,24},{36,28},{40,32... | collective-permute-start | bytes 1671176 | tf_op jit(solution)/shard_map/ppermute | solution.py:113
  24.0 19.5 %collective-permute-start.1 = (bf16[272,1024]{1,0:T(8,128)(2,1)}, bf16[272,1024]{1,0:T(8,128)(2,1)S(1)}, u32[]{:S(2)}, u32[]{:S(2)}) collective-permute-start(bf16[272,1024]{1,0:T(8,128)(2,1)} %get-tuple-element.8), channel_id=1, source_target_pairs={{4,0},{0,4},{12,8},{8,12},{20,16},{16,20},{28,24},{24,28},{36,32},... | collective-permute-start | bytes 1671176 | tf_op jit(solution)/shard_map/ppermute | solution.py:113
  26.0 21.6 %collective-permute-start = (bf16[272,1024]{1,0:T(8,128)(2,1)}, bf16[272,1024]{1,0:T(8,128)(2,1)S(1)}, u32[]{:S(2)}, u32[]{:S(2)}) collective-permute-start(bf16[272,1024]{1,0:T(8,128)(2,1)} %get-tuple-element.8), channel_id=1, source_target_pairs={{500,0},{16,4},{508,8},{24,12},{4,16},{32,20},{12,24},{40,28},{20,... | collective-permute-start | bytes 1671176 | tf_op jit(solution)/shard_map/ppermute | solution.py:113
  36.2 11.4 %collective-permute-start.5 = (bf16[272,1024]{1,0:T(8,128)(2,1)}, bf16[272,1024]{1,0:T(8,128)(2,1)}, u32[]{:S(2)}, u32[]{:S(2)}) collective-permute-start(bf16[272,1024]{1,0:T(8,128)(2,1)} %collective-permute-done.4.behind_ref), channel_id=1, source_target_pairs={{4,0},{0,4},{12,8},{8,12},{20,16},{16,20},{28,24},{24,28},{36,32},... | collective-permute-start | bytes 1671176 | tf_op jit(solution)/shard_map/ppermute | solution.py:113
  39.0 8.6 %collective-permute-start.3 = (bf16[272,1024]{1,0:T(8,128)(2,1)}, bf16[272,1024]{1,0:T(8,128)(2,1)}, u32[]{:S(2)}, u32[]{:S(2)}) collective-permute-start(bf16[272,1024]{1,0:T(8,128)(2,1)} %collective-permute-done.2.ahead_ref), channel_id=1, source_target_pairs={{4,0},{0,4},{12,8},{8,12},{20,16},{16,20},{28,24},{24,28},{36,32},... | collective-permute-start | bytes 1671176 | tf_op jit(solution)/shard_map/ppermute | solution.py:113
  51.6 8.6 %all-to-all-start.1 = ((f32[4,1,256]{2,1,0:T(1,128)}), f32[4,1,256]{2,1,0:T(1,128)S(1)}, u32[]{:S(2)}, u32[]{:S(2)}) async-start(f32[4,1,256]{2,1,0:T(1,128)} %late_maxima.1), calls=%async_computation.1 | async-start | bytes 8192 | tf_op jit(solution)/shard_map/all_to_all | solution.py:167

commit v4 on v3

--- a/solution.py
+++ b/solution.py
@@ -77,33 +77,35 @@
         best[k] = jnp.maximum(best[k], jnp.max(scores + bias, axis=0, keepdims=True))
 
 
-def early_kernel(offset_ref, own_ref, ahead_ref, behind_ref, best_ref):
+def early_kernel(offset_ref, own_ref, mate_ref, ahead_ref, behind_ref, best_ref):
     reps, rows, _ = own_ref.shape
+    odd = lax.rem(lax.axis_index("cluster"), 2)
     best = [jnp.full((1, rows), -4.0, jnp.float32) for _ in range(reps)]
+    score(offset_ref, own_ref, mate_ref, 1 - 2 * odd, best)
     score(offset_ref, own_ref, ahead_ref, jnp.int32(2), best)
     score(offset_ref, own_ref, behind_ref, jnp.int32(-2), best)
     for k in range(reps):
         best_ref[k] = best[k]
 
 
-def late_kernel(
-    offset_ref, own_ref, far_ref, mate_ref, ahead_ref, behind_ref, early_ref, best_ref, ahead, behind, sems
-):
+def late_kernel(offset_ref, own_ref, far_ref, ahead_ref, behind_ref, early_ref, best_ref, behind, ahead, far, sems):
     reps, rows, _ = own_ref.shape
     odd = lax.rem(lax.axis_index("cluster"), 2)
     loads = [
-        pltpu.make_async_copy(ahead_ref, ahead, sems.at[0]),
-        pltpu.make_async_copy(behind_ref, behind, sems.at[1]),
+        pltpu.make_async_copy(behind_ref, behind, sems.at[0]),
+        pltpu.make_async_copy(ahead_ref, ahead, sems.at[1]),
+        pltpu.make_async_copy(far_ref, far, sems.at[2]),
     ]
-    for load in loads:
-        load.start()
+    loads[0].start()
+    loads[1].start()
     best = [early_ref[k] for k in range(reps)]
-    score(offset_ref, own_ref, far_ref, 6 * odd - 3, best)
-    score(offset_ref, own_ref, mate_ref, 1 - 2 * odd, best)
     loads[0].wait()
+    loads[2].start()
+    score(offset_ref, own_ref, behind, -1 - 2 * odd, best)
+    loads[1].wait()
     score(offset_ref, own_ref, ahead, 3 - 2 * odd, best)
-    loads[1].wait()
-    score(offset_ref, own_ref, behind, -1 - 2 * odd, best)
+    loads[2].wait()
+    score(offset_ref, own_ref, far, 6 * odd - 3, best)
     for k in range(reps):
         best_ref[k] = best[k]
 
@@ -146,24 +148,25 @@
     part = pl.pallas_call(
         early_kernel,
         out_shape=part_shape,
-        in_specs=[SMEM] + [VMEM] * 3,
+        in_specs=[SMEM] + [VMEM] * 4,
         out_specs=VMEM,
         name="early_maxima",
         compiler_params=SMALL,
-    )(flat_offsets, own, ahead, behind)
+    )(flat_offsets, own, mate, ahead, behind)
     part = pl.pallas_call(
         late_kernel,
         out_shape=part_shape,
-        in_specs=[SMEM] + [VMEM] * 3 + [HBM] * 2 + [VMEM],
+        in_specs=[SMEM, VMEM] + [HBM] * 3 + [VMEM],
         out_specs=VMEM,
         scratch_shapes=[
             pltpu.VMEM((rows + META, width), jnp.bfloat16),
             pltpu.VMEM((rows + META, width), jnp.bfloat16),
-            pltpu.SemaphoreType.DMA((2,)),
+            pltpu.VMEM((rows + META, width), jnp.bfloat16),
+            pltpu.SemaphoreType.DMA((3,)),
         ],
         name="late_maxima",
         compiler_params=SMALL,
-    )(flat_offsets, own, far, mate, ahead_mate, behind_mate, part)
+    )(flat_offsets, own, far, ahead_mate, behind_mate, part)
     row_best = jnp.max(lax.all_to_all(part, "rep", 0, 0, tiled=True), axis=(0, 1))
     row_ids = lax.axis_index("rep") * rows + jnp.arange(rows, dtype=jnp.int32)
     return jnp.where(row_ids < cluster_sizes[0], row_best, 0.0)

time: 61.3 us -> 61.8 us (level)
  local copies, waits for them, and re-layouts: 0.01 us -> 1.86 us
  waiting for transfers between devices: 14.3 us -> 12.5 us
    unnamed x2 -> x6, local copies, waits for them, and re-layouts: 0.01 us -> 1.86 us
    ppermute x6, waiting for transfers between devices: 10.4 us -> 8.7 us  [over_cluster(): lax.ppermute(block, 'cluster', [((i + (odd if i % 2 else even)) % n, i) f...]
where the time goes in v4:
time: 61.8 us; the launch traced here: 61.3 us
  starting transfers between devices  36 us (58%)
  waiting for transfers between devices  12.5 us (20%)
  Pallas kernels  9.63 us (16%)
  local copies, waits for them, and re-layouts  1.86 us (3%)
  between operations  0.75 us (1%)
    ppermute x6, starting transfers between devices, over_cluster(): lax.ppermute(block, 'cluster', [((i + (odd if i % 2 else even)) % n, i) f...  21.7 us
    all_to_all x1, starting transfers between devices, shards(): own = lax.all_to_all(copies, 'rep', 0, 0, tiled=True)  9.49 us
    ppermute x6, waiting for transfers between devices, over_cluster(): lax.ppermute(block, 'cluster', [((i + (odd if i % 2 else even)) % n, i) f...  8.7 us
    all_to_all x1, starting transfers between devices, shards(): lax.all_to_all(part, 'rep', 0, 0, tiled=True)  4.81 us
    pallas_call x1, Pallas kernels, shards(): pl.pallas_call(late_kernel, out_shape=part_shape, in_specs=[SMEM, VMEM] +...  4.49 us
    all_to_all x1, waiting for transfers between devices, shards(): lax.all_to_all(part, 'rep', 0, 0, tiled=True)  3.83 us
    pallas_call x1, Pallas kernels, shards(): pl.pallas_call(norm_kernel, out_shape=(jax.ShapeDtypeStruct((reps, rows,...  2.75 us
    pallas_call x1, Pallas kernels, shards(): pl.pallas_call(early_kernel, out_shape=part_shape, in_specs=[SMEM] + [VME...  2.39 us
  transfers between devices with their start and end apart: 8, of which 4 were waited for; matrix products, arithmetic and copies ran while one was open for 0% of the time, Pallas kernels for 4%

profile of v4, /device:TPU:2, one launch (start us, length us, event | category | flops | bytes accessed | tf_op | source)
XLA Modules:
  0.0 61.3 jit_solution(926630984956828812)
XLA Ops:
  0.7 2.7 %unit_rows.1 = (bf16[4,256,1024]{2,1,0:T(8,128)(2,1)}, bf16[272,1024]{1,0:T(8,128)(2,1)}) custom-call(s32[1,1]{1,0:T(1,128)} %bitcast.4.size_ref, s32[1,2]{1,0:T(1,128)} %bitcast.5, f32[256,1024]{1,0:T(8,128)} %rows_ref.1), custom_call_target="tpu_custom_call" | custom-call | tf_op jit(solution)/shard_map/unit_rows/pallas_call | solution.py:124
  3.4 0.0 copy-start.2
  3.4 9.5 %all-to-all-start = ((bf16[4,256,1024]{2,1,0:T(8,128)(2,1)}), bf16[4,256,1024]{2,1,0:T(8,128)(2,1)S(1)}, u32[]{:S(2)}, u32[]{:S(2)}) async-start(bf16[4,256,1024]{2,1,0:T(8,128)(2,1)} %get-tuple-element.7), calls=%async_computation | async-start | bytes 4194304 | tf_op jit(solution)/shard_map/all_to_all | solution.py:140
  12.9 1.9 %collective-permute-start.3 = (bf16[272,1024]{1,0:T(8,128)(2,1)}, bf16[272,1024]{1,0:T(8,128)(2,1)S(1)}, u32[]{:S(2)}, u32[]{:S(2)}) collective-permute-start(bf16[272,1024]{1,0:T(8,128)(2,1)} %get-tuple-element.8), channel_id=1, source_target_pairs={{504,0},{508,4},{0,8},{4,12},{8,16},{12,20},{16,24},{20,28},{24,32... | collective-permute-start | bytes 1671176 | tf_op jit(solution)/shard_map/ppermute | solution.py:115
  14.8 9.2 %collective-permute-start.1 = (bf16[272,1024]{1,0:T(8,128)(2,1)}, bf16[272,1024]{1,0:T(8,128)(2,1)S(1)}, u32[]{:S(2)}, u32[]{:S(2)}) collective-permute-start(bf16[272,1024]{1,0:T(8,128)(2,1)} %get-tuple-element.8), channel_id=1, source_target_pairs={{8,0},{12,4},{16,8},{20,12},{24,16},{28,20},{32,24},{36,28},{40,32... | collective-permute-start | bytes 1671176 | tf_op jit(solution)/shard_map/ppermute | solution.py:115
  24.0 1.9 %collective-permute-start.5 = (bf16[272,1024]{1,0:T(8,128)(2,1)}, bf16[272,1024]{1,0:T(8,128)(2,1)S(1)}, u32[]{:S(2)}, u32[]{:S(2)}) collective-permute-start(bf16[272,1024]{1,0:T(8,128)(2,1)} %get-tuple-element.8), channel_id=1, source_target_pairs={{4,0},{0,4},{12,8},{8,12},{20,16},{16,20},{28,24},{24,28},{36,32},... | collective-permute-start | bytes 1671176 | tf_op jit(solution)/shard_map/ppermute | solution.py:115
  26.0 4.8 %collective-permute-start = (bf16[272,1024]{1,0:T(8,128)(2,1)}, bf16[272,1024]{1,0:T(8,128)(2,1)}, u32[]{:S(2)}, u32[]{:S(2)}) collective-permute-start(bf16[272,1024]{1,0:T(8,128)(2,1)} %get-tuple-element.8), channel_id=1, source_target_pairs={{500,0},{16,4},{508,8},{24,12},{4,16},{32,20},{12,24},{40,28},{20,... | collective-permute-start | bytes 1671176 | tf_op jit(solution)/shard_map/ppermute | solution.py:115
  30.8 5.3 %collective-permute-done.3.behind_ref = bf16[272,1024]{1,0:T(8,128)(2,1)S(1)} collective-permute-done((bf16[272,1024]{1,0:T(8,128)(2,1)}, bf16[272,1024]{1,0:T(8,128)(2,1)S(1)}, u32[]{:S(2)}, u32[]{:S(2)}) %collective-permute-start.3) | collective-permute-done | bytes 557088 | tf_op jit(solution)/shard_map/ppermute | solution.py:115
  36.1 1.9 %collective-permute-start.4 = (bf16[272,1024]{1,0:T(8,128)(2,1)S(1)}, bf16[272,1024]{1,0:T(8,128)(2,1)}, u32[]{:S(2)}, u32[]{:S(2)}) collective-permute-start(bf16[272,1024]{1,0:T(8,128)(2,1)S(1)} %collective-permute-done.3.behind_ref), channel_id=1, source_target_pairs={{4,0},{0,4},{12,8},{8,12},{20,16},{16,20},{28,24},{24,28},{36,32},... | collective-permute-start | bytes 1671176 | tf_op jit(solution)/shard_map/ppermute | solution.py:115
  38.0 1.0 %collective-permute-done.1.ahead_ref = bf16[272,1024]{1,0:T(8,128)(2,1)S(1)} collective-permute-done((bf16[272,1024]{1,0:T(8,128)(2,1)}, bf16[272,1024]{1,0:T(8,128)(2,1)S(1)}, u32[]{:S(2)}, u32[]{:S(2)}) %collective-permute-start.1) | collective-permute-done | bytes 557088 | tf_op jit(solution)/shard_map/ppermute | solution.py:115
  39.0 1.9 %collective-permute-start.2 = (bf16[272,1024]{1,0:T(8,128)(2,1)S(1)}, bf16[272,1024]{1,0:T(8,128)(2,1)}, u32[]{:S(2)}, u32[]{:S(2)}) collective-permute-start(bf16[272,1024]{1,0:T(8,128)(2,1)S(1)} %collective-permute-done.1.ahead_ref), channel_id=1, source_target_pairs={{4,0},{0,4},{12,8},{8,12},{20,16},{16,20},{28,24},{24,28},{36,32},... | collective-permute-start | bytes 1671176 | tf_op jit(solution)/shard_map/ppermute | solution.py:115
  41.0 0.0 collective-permute-done.5.mate_ref
  41.0 0.0 copy-start
  41.0 0.8 %copy-done = bf16[272,1024]{1,0:T(8,128)(2,1)} copy-done((bf16[272,1024]{1,0:T(8,128)(2,1)}, bf16[272,1024]{1,0:T(8,128)(2,1)S(1)}, u32[]{:S(2)}) %copy-start) | copy-done | bytes 557080
  41.8 0.0 all-to-all-done.own_ref
  41.8 1.1 %copy-done.1 = bf16[272,1024]{1,0:T(8,128)(2,1)S(1)} copy-done((bf16[272,1024]{1,0:T(8,128)(2,1)S(1)}, bf16[272,1024]{1,0:T(8,128)(2,1)}, u32[]{:S(2)}) %copy-start.1) | copy-done | bytes 557080
  42.8 2.4 %early_maxima.1.early_ref = f32[4,1,256]{2,1,0:T(1,128)S(1)} custom-call(s32[1,2]{1,0:T(1,128)S(1)} %bitcast.6, bf16[4,256,1024]{2,1,0:T(8,128)(2,1)S(1)} %all-to-all-done.own_ref, bf16[272,1024]{1,0:T(8,128)(2,1)S(1)} %copy-done.1, bf16[272,1024]{1,0:T(8,128)(2,1)S(1)} %collective-permute-done.1.ahead_ref, ...), custom_call_target="tpu_custom_call" | custom-call | tf_op jit(solution)/shard_map/early_maxima/pallas_call | solution.py:148
  45.2 2.4 %collective-permute-done.far_ref = bf16[272,1024]{1,0:T(8,128)(2,1)} collective-permute-done((bf16[272,1024]{1,0:T(8,128)(2,1)}, bf16[272,1024]{1,0:T(8,128)(2,1)}, u32[]{:S(2)}, u32[]{:S(2)}) %collective-permute-start) | collective-permute-done | bytes 557088 | tf_op jit(solution)/shard_map/ppermute | solution.py:115
  47.6 0.0 collective-permute-done.4.behind_ref
  47.6 0.0 collective-permute-done.2.ahead_ref
  47.6 4.5 %late_maxima.1 = f32[4,1,256]{2,1,0:T(1,128)} custom-call(s32[1,2]{1,0:T(1,128)S(1)} %bitcast.7, bf16[4,256,1024]{2,1,0:T(8,128)(2,1)S(1)} %all-to-all-done.own_ref, bf16[272,1024]{1,0:T(8,128)(2,1)} %collective-permute-done.far_ref, bf16[272,1024]{1,0:T(8,128)(2,1)} %collective-permute-done.2.ahead_ref, ...), custom_call_target="tpu_custom_call" | custom-call | tf_op jit(solution)/shard_map/late_maxima/pallas_call | solution.py:156
  52.1 4.8 %all-to-all-start.1 = ((f32[4,1,256]{2,1,0:T(1,128)}), f32[4,1,256]{2,1,0:T(1,128)S(1)}, u32[]{:S(2)}, u32[]{:S(2)}) async-start(f32[4,1,256]{2,1,0:T(1,128)} %late_maxima.1), calls=%async_computation.1 | async-start | bytes 8192 | tf_op jit(solution)/shard_map/all_to_all | solution.py:170
  56.9 3.8 %all-to-all-done.1 = f32[4,1,256]{2,1,0:T(1,128)S(1)} async-done(((f32[4,1,256]{2,1,0:T(1,128)}), f32[4,1,256]{2,1,0:T(1,128)S(1)}, u32[]{:S(2)}, u32[]{:S(2)}) %all-to-all-start.1) | async-done | bytes 4128 | tf_op jit(solution)/shard_map/all_to_all | solution.py:170
  60.8 0.6 compare_select_fusion
  (3 shorter events, 0.0 us)
Async XLA Ops:
  3.4 38.4 %copy-start.2 = (s32[2,1]{0,1:T(1,128)S(1)}, s32[2,1]{0,1:T(1,128)}, u32[]{:S(2)}) copy-start(s32[2,1]{0,1:T(1,128)} %param.5) | copy-start | bytes 28
  3.4 38.4 %all-to-all-start = ((bf16[4,256,1024]{2,1,0:T(8,128)(2,1)}), bf16[4,256,1024]{2,1,0:T(8,128)(2,1)S(1)}, u32[]{:S(2)}, u32[]{:S(2)}) async-start(bf16[4,256,1024]{2,1,0:T(8,128)(2,1)} %get-tuple-element.7), calls=%async_computation | async-start | bytes 4194304 | tf_op jit(solution)/shard_map/all_to_all | solution.py:140
  12.9 23.2 %collective-permute-start.3 = (bf16[272,1024]{1,0:T(8,128)(2,1)}, bf16[272,1024]{1,0:T(8,128)(2,1)S(1)}, u32[]{:S(2)}, u32[]{:S(2)}) collective-permute-start(bf16[272,1024]{1,0:T(8,128)(2,1)} %get-tuple-element.8), channel_id=1, source_target_pairs={{504,0},{508,4},{0,8},{4,12},{8,16},{12,20},{16,24},{20,28},{24,32... | collective-permute-start | bytes 1671176 | tf_op jit(solution)/shard_map/ppermute | solution.py:115
  14.8 24.2 %collective-permute-start.1 = (bf16[272,1024]{1,0:T(8,128)(2,1)}, bf16[272,1024]{1,0:T(8,128)(2,1)S(1)}, u32[]{:S(2)}, u32[]{:S(2)}) collective-permute-start(bf16[272,1024]{1,0:T(8,128)(2,1)} %get-tuple-element.8), channel_id=1, source_target_pairs={{8,0},{12,4},{16,8},{20,12},{24,16},{28,20},{32,24},{36,28},{40,32... | collective-permute-start | bytes 1671176 | tf_op jit(solution)/shard_map/ppermute | solution.py:115
  24.0 16.9 %collective-permute-start.5 = (bf16[272,1024]{1,0:T(8,128)(2,1)}, bf16[272,1024]{1,0:T(8,128)(2,1)S(1)}, u32[]{:S(2)}, u32[]{:S(2)}) collective-permute-start(bf16[272,1024]{1,0:T(8,128)(2,1)} %get-tuple-element.8), channel_id=1, source_target_pairs={{4,0},{0,4},{12,8},{8,12},{20,16},{16,20},{28,24},{24,28},{36,32},... | collective-permute-start | bytes 1671176 | tf_op jit(solution)/shard_map/ppermute | solution.py:115
  26.0 21.6 %collective-permute-start = (bf16[272,1024]{1,0:T(8,128)(2,1)}, bf16[272,1024]{1,0:T(8,128)(2,1)}, u32[]{:S(2)}, u32[]{:S(2)}) collective-permute-start(bf16[272,1024]{1,0:T(8,128)(2,1)} %get-tuple-element.8), channel_id=1, source_target_pairs={{500,0},{16,4},{508,8},{24,12},{4,16},{32,20},{12,24},{40,28},{20,... | collective-permute-start | bytes 1671176 | tf_op jit(solution)/shard_map/ppermute | solution.py:115
  36.1 11.5 %collective-permute-start.4 = (bf16[272,1024]{1,0:T(8,128)(2,1)S(1)}, bf16[272,1024]{1,0:T(8,128)(2,1)}, u32[]{:S(2)}, u32[]{:S(2)}) collective-permute-start(bf16[272,1024]{1,0:T(8,128)(2,1)S(1)} %collective-permute-done.3.behind_ref), channel_id=1, source_target_pairs={{4,0},{0,4},{12,8},{8,12},{20,16},{16,20},{28,24},{24,28},{36,32},... | collective-permute-start | bytes 1671176 | tf_op jit(solution)/shard_map/ppermute | solution.py:115
  39.0 8.6 %collective-permute-start.2 = (bf16[272,1024]{1,0:T(8,128)(2,1)S(1)}, bf16[272,1024]{1,0:T(8,128)(2,1)}, u32[]{:S(2)}, u32[]{:S(2)}) collective-permute-start(bf16[272,1024]{1,0:T(8,128)(2,1)S(1)} %collective-permute-done.1.ahead_ref), channel_id=1, source_target_pairs={{4,0},{0,4},{12,8},{8,12},{20,16},{16,20},{28,24},{24,28},{36,32},... | collective-permute-start | bytes 1671176 | tf_op jit(solution)/shard_map/ppermute | solution.py:115
  41.0 0.8 %copy-start = (bf16[272,1024]{1,0:T(8,128)(2,1)}, bf16[272,1024]{1,0:T(8,128)(2,1)S(1)}, u32[]{:S(2)}) copy-start(bf16[272,1024]{1,0:T(8,128)(2,1)S(1)} %collective-permute-done.5.mate_ref) | copy-start | bytes 1671172
  41.8 1.1 %copy-start.1 = (bf16[272,1024]{1,0:T(8,128)(2,1)S(1)}, bf16[272,1024]{1,0:T(8,128)(2,1)}, u32[]{:S(2)}) copy-start(bf16[272,1024]{1,0:T(8,128)(2,1)} %copy-done) | copy-start | bytes 1671172
  52.1 8.6 %all-to-all-start.1 = ((f32[4,1,256]{2,1,0:T(1,128)}), f32[4,1,256]{2,1,0:T(1,128)S(1)}, u32[]{:S(2)}, u32[]{:S(2)}) async-start(f32[4,1,256]{2,1,0:T(1,128)} %late_maxima.1), calls=%async_computation.1 | async-start | bytes 8192 | tf_op jit(solution)/shard_map/all_to_all | solution.py:170

commit v5 on v3

--- a/solution.py
+++ b/solution.py
@@ -97,15 +97,27 @@
     ]
     for load in loads:
         load.start()
-    best = [early_ref[k] for k in range(reps)]
-    score(offset_ref, own_ref, far_ref, 6 * odd - 3, best)
-    score(offset_ref, own_ref, mate_ref, 1 - 2 * odd, best)
+    for k in range(reps):
+        best_ref[k] = early_ref[k]
+
+    def add(payload, delta):
+        paired = delta < 0
+        for k in range(offset_ref.shape[1]):
+            paired = paired | (offset_ref[0, k] == delta)
+
+        @pl.when(paired)
+        def _():
+            best = [best_ref[k] for k in range(reps)]
+            score(offset_ref, own_ref, payload, delta, best)
+            for k in range(reps):
+                best_ref[k] = best[k]
+
+    add(far_ref, 6 * odd - 3)
+    add(mate_ref, 1 - 2 * odd)
     loads[0].wait()
-    score(offset_ref, own_ref, ahead, 3 - 2 * odd, best)
+    add(ahead, 3 - 2 * odd)
     loads[1].wait()
-    score(offset_ref, own_ref, behind, -1 - 2 * odd, best)
-    for k in range(reps):
-        best_ref[k] = best[k]
+    add(behind, -1 - 2 * odd)
 
 
 def over_cluster(block, even, odd):

time: 61.3 us -> 60.7 us (level)
  no operation moved by 1% of the time
where the time goes in v5:
time: 60.7 us; the launch traced here: 60.3 us
  starting transfers between devices  36 us (59%)
  waiting for transfers between devices  14.3 us (24%)
  Pallas kernels  8.73 us (14%)
  between operations  0.76 us (1%)
    ppermute x6, starting transfers between devices, over_cluster(): lax.ppermute(block, 'cluster', [((i + (odd if i % 2 else even)) % n, i) f...  21.7 us
    ppermute x6, waiting for transfers between devices, over_cluster(): lax.ppermute(block, 'cluster', [((i + (odd if i % 2 else even)) % n, i) f...  10.4 us
    all_to_all x1, starting transfers between devices, shards(): own = lax.all_to_all(copies, 'rep', 0, 0, tiled=True)  9.49 us
    all_to_all x1, starting transfers between devices, shards(): lax.all_to_all(part, 'rep', 0, 0, tiled=True)  4.81 us
    all_to_all x1, waiting for transfers between devices, shards(): lax.all_to_all(part, 'rep', 0, 0, tiled=True)  3.83 us
    pallas_call x1, Pallas kernels, shards(): pl.pallas_call(late_kernel, out_shape=part_shape, in_specs=[SMEM] + [VMEM...  3.44 us
    pallas_call x1, Pallas kernels, shards(): pl.pallas_call(norm_kernel, out_shape=(jax.ShapeDtypeStruct((reps, rows,...  2.76 us
    pallas_call x1, Pallas kernels, shards(): pl.pallas_call(early_kernel, out_shape=part_shape, in_specs=[SMEM] + [VME...  2.53 us
  transfers between devices with their start and end apart: 8, of which 4 were waited for; matrix products, arithmetic and copies ran while one was open for 0% of the time, Pallas kernels for 4%

profile of v5, /device:TPU:2, one launch (start us, length us, event | category | flops | bytes accessed | tf_op | source)
XLA Modules:
  0.0 60.3 jit_solution(7881299737074801409)
XLA Ops:
  0.7 2.8 %unit_rows.1 = (bf16[4,256,1024]{2,1,0:T(8,128)(2,1)}, bf16[272,1024]{1,0:T(8,128)(2,1)}) custom-call(s32[1,1]{1,0:T(1,128)} %bitcast.4.size_ref, s32[1,2]{1,0:T(1,128)} %bitcast.5, f32[256,1024]{1,0:T(8,128)} %rows_ref.1), custom_call_target="tpu_custom_call" | custom-call | tf_op jit(solution)/shard_map/unit_rows/pallas_call | solution.py:134
  3.4 0.0 copy-start
  3.4 9.5 %all-to-all-start = ((bf16[4,256,1024]{2,1,0:T(8,128)(2,1)}), bf16[4,256,1024]{2,1,0:T(8,128)(2,1)S(1)}, u32[]{:S(2)}, u32[]{:S(2)}) async-start(bf16[4,256,1024]{2,1,0:T(8,128)(2,1)} %get-tuple-element.7), calls=%async_computation | async-start | bytes 4194304 | tf_op jit(solution)/shard_map/all_to_all | solution.py:150
  12.9 1.9 %collective-permute-start.4 = (bf16[272,1024]{1,0:T(8,128)(2,1)}, bf16[272,1024]{1,0:T(8,128)(2,1)}, u32[]{:S(2)}, u32[]{:S(2)}) collective-permute-start(bf16[272,1024]{1,0:T(8,128)(2,1)} %get-tuple-element.8), channel_id=1, source_target_pairs={{504,0},{508,4},{0,8},{4,12},{8,16},{12,20},{16,24},{20,28},{24,32... | collective-permute-start | bytes 1671176 | tf_op jit(solution)/shard_map/ppermute | solution.py:125
  14.8 9.2 %collective-permute-start.2 = (bf16[272,1024]{1,0:T(8,128)(2,1)}, bf16[272,1024]{1,0:T(8,128)(2,1)}, u32[]{:S(2)}, u32[]{:S(2)}) collective-permute-start(bf16[272,1024]{1,0:T(8,128)(2,1)} %get-tuple-element.8), channel_id=1, source_target_pairs={{8,0},{12,4},{16,8},{20,12},{24,16},{28,20},{32,24},{36,28},{40,32... | collective-permute-start | bytes 1671176 | tf_op jit(solution)/shard_map/ppermute | solution.py:125
  24.0 1.9 %collective-permute-start.1 = (bf16[272,1024]{1,0:T(8,128)(2,1)}, bf16[272,1024]{1,0:T(8,128)(2,1)S(1)}, u32[]{:S(2)}, u32[]{:S(2)}) collective-permute-start(bf16[272,1024]{1,0:T(8,128)(2,1)} %get-tuple-element.8), channel_id=1, source_target_pairs={{4,0},{0,4},{12,8},{8,12},{20,16},{16,20},{28,24},{24,28},{36,32},... | collective-permute-start | bytes 1671176 | tf_op jit(solution)/shard_map/ppermute | solution.py:125
  26.0 4.8 %collective-permute-start = (bf16[272,1024]{1,0:T(8,128)(2,1)}, bf16[272,1024]{1,0:T(8,128)(2,1)S(1)}, u32[]{:S(2)}, u32[]{:S(2)}) collective-permute-start(bf16[272,1024]{1,0:T(8,128)(2,1)} %get-tuple-element.8), channel_id=1, source_target_pairs={{500,0},{16,4},{508,8},{24,12},{4,16},{32,20},{12,24},{40,28},{20,... | collective-permute-start | bytes 1671176 | tf_op jit(solution)/shard_map/ppermute | solution.py:125
  30.8 5.4 %collective-permute-done.4.behind_ref = bf16[272,1024]{1,0:T(8,128)(2,1)} collective-permute-done((bf16[272,1024]{1,0:T(8,128)(2,1)}, bf16[272,1024]{1,0:T(8,128)(2,1)}, u32[]{:S(2)}, u32[]{:S(2)}) %collective-permute-start.4) | collective-permute-done | bytes 557088 | tf_op jit(solution)/shard_map/ppermute | solution.py:125
  36.2 1.9 %collective-permute-start.5 = (bf16[272,1024]{1,0:T(8,128)(2,1)}, bf16[272,1024]{1,0:T(8,128)(2,1)}, u32[]{:S(2)}, u32[]{:S(2)}) collective-permute-start(bf16[272,1024]{1,0:T(8,128)(2,1)} %collective-permute-done.4.behind_ref), channel_id=1, source_target_pairs={{4,0},{0,4},{12,8},{8,12},{20,16},{16,20},{28,24},{24,28},{36,32},... | collective-permute-start | bytes 1671176 | tf_op jit(solution)/shard_map/ppermute | solution.py:125
  38.1 0.9 %collective-permute-done.2.ahead_ref = bf16[272,1024]{1,0:T(8,128)(2,1)} collective-permute-done((bf16[272,1024]{1,0:T(8,128)(2,1)}, bf16[272,1024]{1,0:T(8,128)(2,1)}, u32[]{:S(2)}, u32[]{:S(2)}) %collective-permute-start.2) | collective-permute-done | bytes 557088 | tf_op jit(solution)/shard_map/ppermute | solution.py:125
  39.0 1.9 %collective-permute-start.3 = (bf16[272,1024]{1,0:T(8,128)(2,1)}, bf16[272,1024]{1,0:T(8,128)(2,1)}, u32[]{:S(2)}, u32[]{:S(2)}) collective-permute-start(bf16[272,1024]{1,0:T(8,128)(2,1)} %collective-permute-done.2.ahead_ref), channel_id=1, source_target_pairs={{4,0},{0,4},{12,8},{8,12},{20,16},{16,20},{28,24},{24,28},{36,32},... | collective-permute-start | bytes 1671176 | tf_op jit(solution)/shard_map/ppermute | solution.py:125
  41.0 0.0 all-to-all-done.own_ref
  41.0 0.0 copy-done
  41.0 2.5 %early_maxima.1.early_ref = f32[4,1,256]{2,1,0:T(1,128)S(1)} custom-call(s32[1,2]{1,0:T(1,128)S(1)} %bitcast.6, bf16[4,256,1024]{2,1,0:T(8,128)(2,1)S(1)} %all-to-all-done.own_ref, bf16[272,1024]{1,0:T(8,128)(2,1)} %collective-permute-done.2.ahead_ref, bf16[272,1024]{1,0:T(8,128)(2,1)} %collective-permute-done.4.behind_ref), custom_call_target="tpu_custom_call" | custom-call | tf_op jit(solution)/shard_map/early_maxima/pallas_call | solution.py:158
  43.5 0.0 collective-permute-done.1.mate_ref
  43.5 4.1 %collective-permute-done.far_ref = bf16[272,1024]{1,0:T(8,128)(2,1)S(1)} collective-permute-done((bf16[272,1024]{1,0:T(8,128)(2,1)}, bf16[272,1024]{1,0:T(8,128)(2,1)S(1)}, u32[]{:S(2)}, u32[]{:S(2)}) %collective-permute-start) | collective-permute-done | bytes 557088 | tf_op jit(solution)/shard_map/ppermute | solution.py:125
  47.6 0.0 collective-permute-done.5.behind_ref
  47.6 0.0 collective-permute-done.3.ahead_ref
  47.6 3.4 %late_maxima.1 = f32[4,1,256]{2,1,0:T(1,128)} custom-call(s32[1,2]{1,0:T(1,128)S(1)} %bitcast.7, bf16[4,256,1024]{2,1,0:T(8,128)(2,1)S(1)} %all-to-all-done.own_ref, bf16[272,1024]{1,0:T(8,128)(2,1)S(1)} %collective-permute-done.far_ref, bf16[272,1024]{1,0:T(8,128)(2,1)S(1)} %collective-permute-done.1.mate_ref, ...), custom_call_target="tpu_custom_call" | custom-call | tf_op jit(solution)/shard_map/late_maxima/pallas_call | solution.py:166
  51.1 4.8 %all-to-all-start.1 = ((f32[4,1,256]{2,1,0:T(1,128)}), f32[4,1,256]{2,1,0:T(1,128)S(1)}, u32[]{:S(2)}, u32[]{:S(2)}) async-start(f32[4,1,256]{2,1,0:T(1,128)} %late_maxima.1), calls=%async_computation.1 | async-start | bytes 8192 | tf_op jit(solution)/shard_map/all_to_all | solution.py:179
  55.9 3.8 %all-to-all-done.1 = f32[4,1,256]{2,1,0:T(1,128)S(1)} async-done(((f32[4,1,256]{2,1,0:T(1,128)}), f32[4,1,256]{2,1,0:T(1,128)S(1)}, u32[]{:S(2)}, u32[]{:S(2)}) %all-to-all-start.1) | async-done | bytes 4128 | tf_op jit(solution)/shard_map/all_to_all | solution.py:179
  59.7 0.6 compare_select_fusion
  (1 shorter events, 0.0 us)
Async XLA Ops:
  3.4 37.6 %copy-start = (s32[2,1]{0,1:T(1,128)S(1)}, s32[2,1]{0,1:T(1,128)}, u32[]{:S(2)}) copy-start(s32[2,1]{0,1:T(1,128)} %param.5) | copy-start | bytes 28
  3.4 37.5 %all-to-all-start = ((bf16[4,256,1024]{2,1,0:T(8,128)(2,1)}), bf16[4,256,1024]{2,1,0:T(8,128)(2,1)S(1)}, u32[]{:S(2)}, u32[]{:S(2)}) async-start(bf16[4,256,1024]{2,1,0:T(8,128)(2,1)} %get-tuple-element.7), calls=%async_computation | async-start | bytes 4194304 | tf_op jit(solution)/shard_map/all_to_all | solution.py:150
  12.9 23.3 %collective-permute-start.4 = (bf16[272,1024]{1,0:T(8,128)(2,1)}, bf16[272,1024]{1,0:T(8,128)(2,1)}, u32[]{:S(2)}, u32[]{:S(2)}) collective-permute-start(bf16[272,1024]{1,0:T(8,128)(2,1)} %get-tuple-element.8), channel_id=1, source_target_pairs={{504,0},{508,4},{0,8},{4,12},{8,16},{12,20},{16,24},{20,28},{24,32... | collective-permute-start | bytes 1671176 | tf_op jit(solution)/shard_map/ppermute | solution.py:125
  14.8 24.2 %collective-permute-start.2 = (bf16[272,1024]{1,0:T(8,128)(2,1)}, bf16[272,1024]{1,0:T(8,128)(2,1)}, u32[]{:S(2)}, u32[]{:S(2)}) collective-permute-start(bf16[272,1024]{1,0:T(8,128)(2,1)} %get-tuple-element.8), channel_id=1, source_target_pairs={{8,0},{12,4},{16,8},{20,12},{24,16},{28,20},{32,24},{36,28},{40,32... | collective-permute-start | bytes 1671176 | tf_op jit(solution)/shard_map/ppermute | solution.py:125
  24.0 19.5 %collective-permute-start.1 = (bf16[272,1024]{1,0:T(8,128)(2,1)}, bf16[272,1024]{1,0:T(8,128)(2,1)S(1)}, u32[]{:S(2)}, u32[]{:S(2)}) collective-permute-start(bf16[272,1024]{1,0:T(8,128)(2,1)} %get-tuple-element.8), channel_id=1, source_target_pairs={{4,0},{0,4},{12,8},{8,12},{20,16},{16,20},{28,24},{24,28},{36,32},... | collective-permute-start | bytes 1671176 | tf_op jit(solution)/shard_map/ppermute | solution.py:125
  26.0 21.6 %collective-permute-start = (bf16[272,1024]{1,0:T(8,128)(2,1)}, bf16[272,1024]{1,0:T(8,128)(2,1)S(1)}, u32[]{:S(2)}, u32[]{:S(2)}) collective-permute-start(bf16[272,1024]{1,0:T(8,128)(2,1)} %get-tuple-element.8), channel_id=1, source_target_pairs={{500,0},{16,4},{508,8},{24,12},{4,16},{32,20},{12,24},{40,28},{20,... | collective-permute-start | bytes 1671176 | tf_op jit(solution)/shard_map/ppermute | solution.py:125
  36.2 11.4 %collective-permute-start.5 = (bf16[272,1024]{1,0:T(8,128)(2,1)}, bf16[272,1024]{1,0:T(8,128)(2,1)}, u32[]{:S(2)}, u32[]{:S(2)}) collective-permute-start(bf16[272,1024]{1,0:T(8,128)(2,1)} %collective-permute-done.4.behind_ref), channel_id=1, source_target_pairs={{4,0},{0,4},{12,8},{8,12},{20,16},{16,20},{28,24},{24,28},{36,32},... | collective-permute-start | bytes 1671176 | tf_op jit(solution)/shard_map/ppermute | solution.py:125
  39.0 8.6 %collective-permute-start.3 = (bf16[272,1024]{1,0:T(8,128)(2,1)}, bf16[272,1024]{1,0:T(8,128)(2,1)}, u32[]{:S(2)}, u32[]{:S(2)}) collective-permute-start(bf16[272,1024]{1,0:T(8,128)(2,1)} %collective-permute-done.2.ahead_ref), channel_id=1, source_target_pairs={{4,0},{0,4},{12,8},{8,12},{20,16},{16,20},{28,24},{24,28},{36,32},... | collective-permute-start | bytes 1671176 | tf_op jit(solution)/shard_map/ppermute | solution.py:125
  51.1 8.6 %all-to-all-start.1 = ((f32[4,1,256]{2,1,0:T(1,128)}), f32[4,1,256]{2,1,0:T(1,128)S(1)}, u32[]{:S(2)}, u32[]{:S(2)}) async-start(f32[4,1,256]{2,1,0:T(1,128)} %late_maxima.1), calls=%async_computation.1 | async-start | bytes 8192 | tf_op jit(solution)/shard_map/all_to_all | solution.py:179
